TPU v7x, 32 devices: a whole 2x2x4 slice. The times are simulated.
32 devices in a mesh: seq: 16 (over z, y, x), chan: 2 (over core).
Axes of the slice: x: 2, y: 2, z: 4, core: 2. Of those that a mesh axis runs over, the one named last changes fastest.
Arguments:
- hyena_gate: bfloat16 [8192, 4096], P('seq', 'chan'), may hold values from -6 to 6
- hyena_key: bfloat16 [8192, 4096], P('seq', 'chan'), may hold values from -6 to 6
- hyena_value: bfloat16 [8192, 4096], P('seq', 'chan'), may hold values from -6 to 6
- long_filter: bfloat16 [8192, 4096], P('seq', 'chan'), may hold values from -0.0625 to 0.0625
- skip_weight: float32 [4096], P('chan'), may hold values from -4 to 4
- attn_query: bfloat16 [8192, 8, 1024], P('seq', 'chan'), may hold values from -4.5 to 4.5
- attn_keys: bfloat16 [8192, 1024], P('seq', 'chan'), may hold values from -4.5 to 4.5
- attn_values: bfloat16 [8192, 1024], P('seq', 'chan'), may hold values from -6 to 6
Outputs:
- hyena_out: bfloat16 [8192, 4096], P('seq', 'chan')
- attn_out: bfloat16 [8192, 8, 1024], P('seq', 'chan')
- attn_lse: float32 [8, 8, 8192], P('chan', None, 'seq')
All inputs are finite; a program needn't handle non-finite values.
Results may differ from a plain program's by a relative error of at most 0.0045.
Values may be sent and summed in bfloat16 or wider, within the bound.
A program may use at most 192 MiB of HBM per device.

v0:
```python
import math

import jax
import jax.numpy as jnp
from jax import lax
from jax.sharding import PartitionSpec as P

KVH = 8
HD = 128


PRECISE = lax.Precision.HIGHEST


def from_behind(x, axis, by):
    devices = lax.axis_size(axis)
    pairs = [(i, i + by) for i in range(devices) if 0 <= i + by < devices]
    return lax.ppermute(x, axis, pairs)


def wave_table(row_ids, col_ids, period):
    phase = row_ids[:, None] * col_ids[None, :] % period
    angles = phase.astype(jnp.float32) * (2.0 * math.pi / period)
    return (jnp.cos(angles), jnp.sin(angles))


def pair_order(shard_count):
    first_half = jnp.arange(shard_count, dtype=jnp.int32)
    partner = jnp.where(first_half == 0, shard_count, 2 * shard_count - first_half)
    return jnp.stack([first_half, partner], axis=1).reshape(-1)


def line_transform(real_part, imag_part, sign):
    length = real_part.shape[1]
    index = jnp.arange(length, dtype=jnp.int32)
    line_cos, line_sin = wave_table(index, index, length)
    cos_re = jnp.einsum("da,cak->cdk", line_cos, real_part, precision=PRECISE)
    cos_im = jnp.einsum("da,cak->cdk", line_cos, imag_part, precision=PRECISE)
    sin_re = jnp.einsum("da,cak->cdk", line_sin, real_part, precision=PRECISE)
    sin_im = jnp.einsum("da,cak->cdk", line_sin, imag_part, precision=PRECISE)
    return (cos_re + sign * sin_im, cos_im - sign * sin_re)


def long_conv(signal, kernel):
    shard_count = lax.axis_size("seq")
    my_index = lax.axis_index("seq")
    length, channels = signal.shape
    piece_len = length // shard_count
    full_span = 2 * shard_count * length
    freq_order = pair_order(shard_count)
    stacked = jnp.concatenate([signal, kernel], axis=1).reshape(
        shard_count, piece_len, 2 * channels
    )
    blocks = lax.all_to_all(stacked, "seq", split_axis=0, concat_axis=0, tiled=True)
    first_cos, first_sin = wave_table(
        freq_order, jnp.arange(shard_count, dtype=jnp.int32), 2 * shard_count
    )
    spread_re = jnp.einsum("cb,bwk->cwk", first_cos, blocks, precision=PRECISE)
    spread_im = -jnp.einsum("cb,bwk->cwk", first_sin, blocks, precision=PRECISE)
    positions = my_index * piece_len + jnp.arange(piece_len, dtype=jnp.int32)
    twist_cos, twist_sin = wave_table(freq_order, positions, full_span)
    twist_cos = twist_cos[:, :, None]
    twist_sin = twist_sin[:, :, None]
    turned_re = spread_re * twist_cos + spread_im * twist_sin
    turned_im = spread_im * twist_cos - spread_re * twist_sin
    recv_re, recv_im = (
        lax.all_to_all(turned_re, "seq", split_axis=0, concat_axis=1, tiled=True),
        lax.all_to_all(turned_im, "seq", split_axis=0, concat_axis=1, tiled=True),
    )
    full_re, full_im = line_transform(recv_re, recv_im, 1.0)
    sig_re = full_re[..., :channels]
    sig_im = full_im[..., :channels]
    ker_re = full_re[..., channels:]
    ker_im = full_im[..., channels:]
    prod_re = sig_re * ker_re - sig_im * ker_im
    prod_im = sig_re * ker_im + sig_im * ker_re
    back_re, back_im = line_transform(prod_re, prod_im, -1.0)
    slot_freq = jnp.stack(
        [my_index, jnp.where(my_index == 0, shard_count, 2 * shard_count - my_index)]
    )
    back_cos, back_sin = wave_table(slot_freq, jnp.arange(length, dtype=jnp.int32), full_span)
    back_cos = back_cos[:, :, None]
    back_sin = back_sin[:, :, None]
    reverted_re = back_re * back_cos - back_im * back_sin
    reverted_im = back_im * back_cos + back_re * back_sin
    final_re, final_im = (
        lax.all_to_all(reverted_re, "seq", split_axis=1, concat_axis=0, tiled=True),
        lax.all_to_all(reverted_im, "seq", split_axis=1, concat_axis=0, tiled=True),
    )
    last_cos, last_sin = wave_table(
        jnp.arange(shard_count, dtype=jnp.int32), freq_order, 2 * shard_count
    )
    values = jnp.einsum("bc,cwk->bwk", last_cos, final_re, precision=PRECISE)
    values = values - jnp.einsum("bc,cwk->bwk", last_sin, final_im, precision=PRECISE)
    values = values * (1.0 / full_span)
    placed = lax.all_to_all(values, "seq", split_axis=0, concat_axis=1, tiled=True)
    return placed.reshape(length, channels)


def attend(attn_query, window, my_index):
    tokens, groups, features = attn_query.shape
    queries = attn_query.reshape(tokens, groups, KVH, HD)
    key_rows = window[0].reshape(2 * tokens, KVH, HD)
    value_rows = window[1].reshape(2 * tokens, KVH, HD)
    scores = jnp.einsum(
        "tgjd,sjd->gjts", queries, key_rows, preferred_element_type=jnp.float32
    ) * HD ** (-0.5)
    key_pos = jnp.arange(2 * tokens, dtype=jnp.int32) - tokens
    query_pos = jnp.arange(tokens, dtype=jnp.int32)
    allowed = (key_pos[None, :] <= query_pos[:, None]) & ((key_pos[None, :] >= 0) | (my_index > 0))
    scores = jnp.where(allowed, scores, jnp.float32(-1e30))
    row_peak = jnp.max(scores, axis=-1)
    expd = jnp.exp(scores - row_peak[..., None])
    row_total = jnp.sum(expd, axis=-1)
    weights = expd.astype(jnp.bfloat16)
    mixed_sum = jnp.einsum(
        "gjts,sjd->tgjd", weights, value_rows, preferred_element_type=jnp.float32
    )
    normed = mixed_sum / row_total.transpose(2, 0, 1)[..., None]
    return (
        normed.astype(jnp.bfloat16).reshape(tokens, groups, features),
        row_peak + jnp.log(row_total),
    )


def local(
    hyena_gate, hyena_key, hyena_value, long_filter, skip_weight, attn_query, attn_keys, attn_values
):
    my_index = lax.axis_index("seq")
    signal = hyena_key.astype(jnp.float32) * hyena_value.astype(jnp.float32)
    kv_pair = jnp.stack([attn_keys, attn_values])
    all_heads = lax.all_gather(kv_pair, "chan", axis=2, tiled=True)
    behind = from_behind(all_heads, "seq", 1)
    window = jnp.concatenate([behind, all_heads], axis=1)
    conv = long_conv(signal, long_filter.astype(jnp.float32))
    hyena_out = (hyena_gate.astype(jnp.float32) * (conv + skip_weight * signal)).astype(
        jnp.bfloat16
    )
    attn_out, attn_lse = attend(attn_query, window, my_index)
    return (hyena_out, attn_out, attn_lse)


def solution(mesh):
    return jax.shard_map(
        local,
        mesh=mesh,
        in_specs=(
            P("seq", "chan"),
            P("seq", "chan"),
            P("seq", "chan"),
            P("seq", "chan"),
            P("chan"),
            P("seq", "chan", None),
            P("seq", "chan"),
            P("seq", "chan"),
        ),
        out_specs=(P("seq", "chan"), P("seq", "chan", None), P("chan", None, "seq")),
        check_vma=False,
    )
```

profile of v0, /device:TPU:12, one launch (start us, length us, event | category | flops | bytes accessed | tf_op | source)
XLA Modules:
  0.0 2036.5 jit_solution(5671530889849337863)
XLA Ops:
  23.7 188.3 %all-to-all-done = f32[16,32,4096]{2,1,0:T(8,128)} async-done(((f32[16,32,4096]{2,1,0:T(8,128)}), f32[16,32,4096]{2,1,0:T(8,128)}, u32[]{:S(2)}, u32[]{:S(2)}) %all-to-all-start) | async-done | bytes 8388640 | tf_op jit(solution)/shard_map/all_to_all | solution.py:54
  212.0 20.5 %fusion.7 = f32[32,32,4096]{2,0,1:T(8,128)S(1)} fusion(f32[16,32,4096]{2,1,0:T(8,128)} %all-to-all-done, s32[32]{0:T(128)S(1)} %mul.299), kind=kOutput, calls=%fused_computation.20 | convolution fusion | flops 805313536 | bytes 25165952 | tf_op jit(solution)/shard_map/cb,bwk->cwk/dot_general | solution.py:59
  232.5 26.7 %multiply_add_fusion = (f32[32,32,4096]{2,0,1:T(8,128)}, f32[32,32,4096]{2,0,1:T(8,128)}) fusion(f32[32,32,4096]{2,0,1:T(8,128)S(1)} %fusion.7, f32[32,32]{0,1:T(8,128)S(1)} %get-tuple-element.21, f32[32,32]{0,1:T(8,128)S(1)} %get-tuple-element.20, f32[16,32,4096]{2,1,0:T(8,128)} %all-to-all-done, s32[32]{0:T(128)S(1)} %mul.299), kind=kOutput, calls=%fused_computation.10 | convolution fusion | flops 834673664 | bytes 58728576 | tf_op jit(solution)/shard_map/cb,bwk->cwk/dot_general | solution.py:58
  259.2 18.0 copy.68
  284.7 17.7 copy.71
  302.4 359.1 %all-to-all-done.1 = f32[32,32,4096]{2,1,0:T(8,128)} async-done(((f32[32,32,4096]{2,1,0:T(8,128)}), f32[32,32,4096]{2,1,0:T(8,128)}, u32[]{:S(2)}, u32[]{:S(2)}) %all-to-all-start.1) | async-done | bytes 16777248 | tf_op jit(solution)/shard_map/all_to_all | solution.py:67
  682.5 85.0 %fusion.31 = f32[2,4096,512]{2,1,0:T(8,128)} fusion(f32[2,512,4096]{2,1,0:T(8,128)S(1)} %bitcast.113), kind=kOutput, calls=%fused_computation.50 | convolution fusion | flops 25773473792 | bytes 33554432 | tf_op jit(solution)/shard_map/da,cak->cdk/dot_general | solution.py:37
  767.5 276.9 %all-to-all-done.2 = f32[32,32,4096]{2,1,0:T(8,128)} async-done(((f32[32,32,4096]{2,1,0:T(8,128)}), f32[32,32,4096]{2,1,0:T(8,128)}, u32[]{:S(2)}, u32[]{:S(2)}) %all-to-all-start.2) | async-done | bytes 16777248 | tf_op jit(solution)/shard_map/all_to_all | solution.py:68
  1056.8 69.8 %fusion.29 = f32[2,4096,512]{2,1,0:T(8,128)} fusion(f32[2,512,4096]{2,1,0:T(8,128)S(1)} %bitcast.117), kind=kOutput, calls=%fused_computation.48 | convolution fusion | flops 25773473792 | bytes 33554432 | tf_op jit(solution)/shard_map/da,cak->cdk/dot_general | solution.py:38
  1126.6 73.4 %add_bitcast_fusion = f32[2,512,4096]{1,2,0:T(8,128)} fusion(f32[2,4096,512]{2,1,0:T(8,128)} %fusion.31, f32[2,512,4096]{2,1,0:T(8,128)} %bitcast.118), kind=kOutput, calls=%fused_computation.8 | convolution fusion | flops 25777668096 | bytes 50331648 | tf_op jit(solution)/shard_map/da,cak->cdk/dot_general | solution.py:40
  1200.1 71.7 %subtract_bitcast_fusion = f32[2,512,4096]{1,2,0:T(8,128)} fusion(f32[2,4096,512]{2,1,0:T(8,128)} %fusion.29, f32[2,512,4096]{2,1,0:T(8,128)S(1)} %bitcast.116), kind=kOutput, calls=%fused_computation.7 | convolution fusion | flops 25777668096 | bytes 50331648 | tf_op jit(solution)/shard_map/da,cak->cdk/dot_general | solution.py:39
  1271.8 19.3 multiply_subtract_fusion.2
  1291.2 26.0 %fusion.27 = f32[2,2048,512]{2,1,0:T(8,128)} fusion(f32[2,512,2048]{1,2,0:T(8,128)} %get-tuple-element.14), kind=kOutput, calls=%fused_computation.46 | convolution fusion | flops 12888571904 | bytes 16777216 | tf_op jit(solution)/shard_map/da,cak->cdk/dot_general | solution.py:37
  1317.2 17.4 fusion.25
  1334.6 23.4 %multiply_subtract_fusion.1 = f32[2,2048,512]{2,1,0:T(8,128)} fusion(f32[2,2048,512]{2,1,0:T(8,128)S(1)} %fusion.25, f32[2,512,2048]{1,2,0:T(8,128)S(1)} %bitcast.120), kind=kOutput, calls=%fused_computation.16 | convolution fusion | flops 12892766208 | bytes 25165824 | tf_op jit(solution)/shard_map/da,cak->cdk/dot_general | solution.py:39
  1358.0 28.5 %add_bitcast_fusion.1 = (f32[2,512,2048]{1,2,0:T(8,128)}, f32[2,512,2048]{1,2,0:T(8,128)}) fusion(f32[2,2048,512]{2,1,0:T(8,128)} %multiply_subtract_fusion.1, f32[2,512]{1,0:T(2,128)S(1)} %get-tuple-element.23, f32[2,512]{1,0:T(2,128)S(1)} %get-tuple-element.22, f32[2,2048,512]{2,1,0:T(8,128)} %fusion.27, f32[2,512,2048]{1,2,0:T(8,128)} %get-tuple-element.15), kind=kOutput, calls=%fused_computation.14 | convolution fusion | flops 12905349120 | bytes 41951232 | tf_op jit(solution)/shard_map/da,cak->cdk/dot_general | solution.py:40
  1386.6 13.4 copy.79
  1400.0 8.7 all-to-all-start.4
  1408.7 13.4 copy.76
  1422.1 165.9 %all-to-all-done.4 = f32[2,512,2048]{2,0,1:T(2,128)} async-done(((f32[2,512,2048]{2,0,1:T(2,128)}), f32[2,512,2048]{2,0,1:T(2,128)}, u32[]{:S(2)}, u32[]{:S(2)}) %all-to-all-start.4) | async-done | bytes 8388640 | tf_op jit(solution)/shard_map/all_to_all | solution.py:88
  1595.3 13.1 all-gather.2.cloned.1.call-done
  1620.4 98.1 %collective-permute-done = bf16[2,512,1024]{1,2,0:T(8,128)(2,1)} collective-permute-done((bf16[2,512,1024]{1,2,0:T(8,128)(2,1)}, bf16[2,512,1024]{1,2,0:T(8,128)(2,1)}, u32[]{:S(2)}, u32[]{:S(2)}) %collective-permute-start) | collective-permute-done | bytes 2097184 | tf_op jit(solution)/shard_map/ppermute | solution.py:18
  1722.4 24.5 %fusion.2 = (f32[4,8,512]{2,0,1:T(4,128)S(1)}, f32[8,1024,512,4]{2,1,3,0:T(8,128)}) fusion(pred[512,1024]{0,1:T(8,128)(4,1)S(1)} %fusion.17, bf16[1024,8,128,1]{0,2,3,1:T(8,128)(2,1)S(1)} %bitcast.125, bf16[512,4,8,128]{3,2,1,0:T(8,128)(2,1)S(1)} %copy-done.3), kind=kOutput, calls=%fused_computation.4 | convolution fusion | flops 4345282560 | bytes 73990144 | tf_op jit(solution)/shard_map/tgjd,sjd->gjts/dot_general | solution.py:105
  1755.1 8.7 copy.81
  1763.8 11.1 all_to_all.78
  1774.8 25.3 %all-to-all-done.3 = f32[2,512,2048]{2,0,1:T(2,128)} async-done(((f32[2,512,2048]{2,0,1:T(2,128)}), f32[2,512,2048]{2,0,1:T(2,128)}, u32[]{:S(2)}, u32[]{:S(2)}) %all-to-all-start.3) | async-done | bytes 8388640 | tf_op jit(solution)/shard_map/all_to_all | solution.py:87
  1808.3 8.7 copy.78
  1817.0 10.9 all_to_all.74
  1846.0 85.9 %all-to-all-start.5 = ((f32[16,32,2048]{2,1,0:T(8,128)}), f32[16,32,2048]{2,1,0:T(8,128)}, u32[]{:S(2)}, u32[]{:S(2)}) async-start(f32[16,32,2048]{2,1,0:T(8,128)} %copy.82), calls=%async_computation.5 | async-start | bytes 8388608 | tf_op jit(solution)/shard_map/all_to_all | solution.py:96
  1931.9 21.8 %fusion = f32[4,8,512]{2,0,1:T(4,128)S(1)} fusion(f32[8,1024,512,4]{2,1,3,0:T(8,128)} %get-tuple-element.25, f32[4,8,512]{2,0,1:T(4,128)S(1)} %get-tuple-element.24, pred[512,1024]{0,1:T(8,128)(4,1)S(1)} %fusion.17), kind=kLoop, calls=%fused_computation.2 | loop fusion | flops 67092480 | bytes 67764224 | tf_op jit(solution)/shard_map/reduce_sum | solution.py:114
  1953.7 27.6 %fusion.6 = bf16[512,4,8,128]{0,3,1,2:T(8,128)(2,1)} fusion(f32[512,4,8]{0,1,2:T(4,128)S(1)} %bitcast.131, bf16[1024,8,128,1]{0,2,3,1:T(8,128)(2,1)S(1)} %bitcast.128, f32[8,1024,512,4]{2,1,3,0:T(8,128)} %get-tuple-element.25, f32[4,8,512]{2,0,1:T(4,128)S(1)} %get-tuple-element.24, pred[512,1024]{0,1:T(8,128)(4,1)S(1)} %fusion.17), kind=kOutput, calls=%fused_computation.13 | convolution fusion | flops 4366270464 | bytes 74055680 | tf_op jit(solution)/shard_map/gjts,sjd->tgjd/dot_general | solution.py:116
  1994.7 28.5 %all-to-all-done.5 = f32[16,32,2048]{2,1,0:T(8,128)} async-done(((f32[16,32,2048]{2,1,0:T(8,128)}), f32[16,32,2048]{2,1,0:T(8,128)}, u32[]{:S(2)}, u32[]{:S(2)}) %all-to-all-start.5) | async-done | bytes 4194336 | tf_op jit(solution)/shard_map/all_to_all | solution.py:96
  (79 shorter events, 134.7 us)
Async XLA Ops:
  16.1 195.8 %all-to-all-start = ((f32[16,32,4096]{2,1,0:T(8,128)}), f32[16,32,4096]{2,1,0:T(8,128)}, u32[]{:S(2)}, u32[]{:S(2)}) async-start(f32[16,32,4096]{2,1,0:T(8,128)} %bitcast.121), calls=%async_computation | async-start | bytes 16777216 | tf_op jit(solution)/shard_map/all_to_all | solution.py:54
  23.5 208.9 %copy-start.9 = (s32[32]{0:T(128)}, s32[32]{0:T(128)S(1)}, u32[]{:S(2)}) copy-start(s32[32]{0:T(128)S(1)} %mul.299) | copy-start | bytes 388
  277.2 384.3 %all-to-all-start.1 = ((f32[32,32,4096]{2,1,0:T(8,128)}), f32[32,32,4096]{2,1,0:T(8,128)}, u32[]{:S(2)}, u32[]{:S(2)}) async-start(f32[32,32,4096]{2,1,0:T(8,128)} %copy.68), calls=%async_computation.1 | async-start | bytes 33554432 | tf_op jit(solution)/shard_map/all_to_all | solution.py:67
  661.5 382.9 %all-to-all-start.2 = ((f32[32,32,4096]{2,1,0:T(8,128)}), f32[32,32,4096]{2,1,0:T(8,128)}, u32[]{:S(2)}, u32[]{:S(2)}) async-start(f32[32,32,4096]{2,1,0:T(8,128)} %copy.71), calls=%async_computation.2 | async-start | bytes 33554432 | tf_op jit(solution)/shard_map/all_to_all | solution.py:68
  676.8 5.8 copy-start
  1051.1 5.8 copy-start.1
  1056.8 143.2 %slice-start = ((s8[16777216]{0:T(1024)(128)(4,1)}), s8[4194304]{0:T(1024)(128)(4,1)S(1)}, s32[]{:S(2)}) async-start(s8[16777216]{0:T(1024)(128)(4,1)} %bitcast.114), calls=%async_computation.7 | async-start | bytes 8388608
  1056.8 143.2 %slice-start.1 = ((s8[16777216]{0:T(1024)(128)(4,1)}), s8[4194304]{0:T(1024)(128)(4,1)S(1)}, s32[]{:S(2)}) async-start(s8[16777216]{0:T(1024)(128)(4,1)} %bitcast.114), calls=%async_computation.8 | async-start | bytes 8388608
  1126.6 73.4 %slice-start.2 = ((s8[16777216]{0:T(1024)(128)(4,1)}), s8[4194304]{0:T(1024)(128)(4,1)S(1)}, s32[]{:S(2)}) async-start(s8[16777216]{0:T(1024)(128)(4,1)} %bitcast.114), calls=%async_computation.9 | async-start | bytes 8388608
  1126.6 73.4 %slice-start.3 = ((s8[16777216]{0:T(1024)(128)(4,1)}), s8[4194304]{0:T(1024)(128)(4,1)S(1)}, s32[]{:S(2)}) async-start(s8[16777216]{0:T(1024)(128)(4,1)} %bitcast.114), calls=%async_computation.10 | async-start | bytes 8388608
  1291.2 26.0 %copy-start.2 = (f32[2,512,2048]{1,2,0:T(8,128)S(1)}, f32[2,512,2048]{1,2,0:T(8,128)}, u32[]{:S(2)}) copy-start(f32[2,512,2048]{1,2,0:T(8,128)} %get-tuple-element.15) | copy-start | bytes 25165828
  1291.2 43.5 %slice-start.4 = ((s8[8388608]{0:T(1024)(128)(4,1)}), s8[4194304]{0:T(1024)(128)(4,1)S(1)}, s32[]{:S(2)}) async-start(s8[8388608]{0:T(1024)(128)(4,1)} %bitcast.119), calls=%async_computation.11 | async-start | bytes 8388608
  1317.2 17.5 slice-start.5
  1400.0 188.0 %all-to-all-start.4 = ((f32[2,512,2048]{2,0,1:T(2,128)}), f32[2,512,2048]{2,0,1:T(2,128)}, u32[]{:S(2)}, u32[]{:S(2)}) async-start(f32[2,512,2048]{2,0,1:T(2,128)} %copy.79), calls=%async_computation.4 | async-start | bytes 16777216 | tf_op jit(solution)/shard_map/all_to_all | solution.py:88
  1422.1 171.7 %copy-start.7 = (bf16[512,512]{1,0:T(8,128)(2,1)S(1)}, bf16[512,512]{1,0:T(8,128)(2,1)}, u32[]{:S(2)}) copy-start(bf16[512,512]{1,0:T(8,128)(2,1)} %param.14) | copy-start | bytes 1572868
  1422.1 171.9 %copy-start.8 = (bf16[512,512]{1,0:T(8,128)(2,1)S(1)}, bf16[512,512]{1,0:T(8,128)(2,1)}, u32[]{:S(2)}) copy-start(bf16[512,512]{1,0:T(8,128)(2,1)} %param.15) | copy-start | bytes 1572868
  1588.0 212.1 %all-to-all-start.3 = ((f32[2,512,2048]{2,0,1:T(2,128)}), f32[2,512,2048]{2,0,1:T(2,128)}, u32[]{:S(2)}, u32[]{:S(2)}) async-start(f32[2,512,2048]{2,0,1:T(2,128)} %copy.76), calls=%async_computation.3 | async-start | bytes 16777216 | tf_op jit(solution)/shard_map/all_to_all | solution.py:87
  1593.7 14.7 all-gather.2.cloned.1.call-start
  1608.4 111.9 %copy-start.5 = (bf16[2,512,1024]{1,2,0:T(8,128)(2,1)S(1)}, bf16[2,512,1024]{1,2,0:T(8,128)(2,1)}, u32[]{:S(2)}) copy-start(bf16[2,512,1024]{1,2,0:T(8,128)(2,1)} %all-gather.2.cloned.1.call-done) | copy-start | bytes 6291460
  1608.4 110.1 %collective-permute-start = (bf16[2,512,1024]{1,2,0:T(8,128)(2,1)}, bf16[2,512,1024]{1,2,0:T(8,128)(2,1)}, u32[]{:S(2)}, u32[]{:S(2)}) collective-permute-start(bf16[2,512,1024]{1,2,0:T(8,128)(2,1)} %all-gather.2.cloned.1.call-done), channel_id=1, source_target_pairs={{0,2},{2,4},{4,6},{6,8},{8,10},{10,12},{12,14},{14,16},{16,18},{18... | collective-permute-start | bytes 6291464 | tf_op jit(solution)/shard_map/ppermute | solution.py:18
  1620.4 102.0 %copy-start.3 = (bf16[512,4,8,128]{3,2,1,0:T(8,128)(2,1)S(1)}, bf16[512,4,8,128]{3,2,1,0:T(8,128)(2,1)}, u32[]{:S(2)}) copy-start(bf16[512,4,8,128]{3,2,1,0:T(8,128)(2,1)} %reshape.186) | copy-start | bytes 12582916
  1817.0 10.9 copy-start.10
  1846.0 177.2 %all-to-all-start.5 = ((f32[16,32,2048]{2,1,0:T(8,128)}), f32[16,32,2048]{2,1,0:T(8,128)}, u32[]{:S(2)}, u32[]{:S(2)}) async-start(f32[16,32,2048]{2,1,0:T(8,128)} %copy.82), calls=%async_computation.5 | async-start | bytes 8388608 | tf_op jit(solution)/shard_map/all_to_all | solution.py:96
  1931.9 21.8 %copy-start.6 = (bf16[1,1024,1024]{1,2,0:T(8,128)(2,1)S(1)}, bf16[1,1024,1024]{1,2,0:T(8,128)(2,1)}, u32[]{:S(2)}) copy-start(bf16[1,1024,1024]{1,2,0:T(8,128)(2,1)} %get-tuple-element.18) | copy-start | bytes 6291460
  1981.3 41.9 %copy-start.4 = (bf16[512,2048]{1,0:T(8,128)(2,1)S(1)}, bf16[512,2048]{1,0:T(8,128)(2,1)}, u32[]{:S(2)}) copy-start(bf16[512,2048]{1,0:T(8,128)(2,1)} %param.10) | copy-start | bytes 6291460
  1981.3 41.9 %copy-start.11 = (f32[2048]{0:T(1024)S(1)}, f32[2048]{0:T(1024)}, u32[]{:S(2)}) copy-start(f32[2048]{0:T(1024)} %param.12) | copy-start | bytes 24580
Sparse Core Ops, SparseCore 0:
  1596.7 11.6 all-gather.1
where the time goes:
time: 2050 us; the launch traced here: 2040 us
  waiting for transfers between devices  1160 us (57%)
  matrix products  508 us (25%)
  local copies, waits for them, and re-layouts  173 us (8%)
  starting transfers between devices  127 us (6%)
  other arithmetic  58.7 us (3%)
    all_to_all x1, waiting for transfers between devices, long_conv(): lax.all_to_all(turned_re, 'seq', split_axis=0, concat_axis=1, tiled=True)  359 us
    all_to_all x1, waiting for transfers between devices, long_conv(): lax.all_to_all(turned_im, 'seq', split_axis=0, concat_axis=1, tiled=True)  277 us
    all_to_all x1, waiting for transfers between devices, long_conv(): lax.all_to_all(stacked, 'seq', split_axis=0, concat_axis=0, tiled=True)  188 us
    all_to_all x1, waiting for transfers between devices, long_conv(): lax.all_to_all(reverted_im, 'seq', split_axis=1, concat_axis=0, tiled=True)  166 us
    dot_general x2, matrix products, line_transform(): cos_re = jnp.einsum('da,cak->cdk', line_cos, real_part, precision=PRECISE)  111 us
    dot_general x2, matrix products, line_transform(): sin_im = jnp.einsum('da,cak->cdk', line_sin, imag_part, precision=PRECISE)  102 us
    ppermute x1, waiting for transfers between devices, from_behind(): return lax.ppermute(x, axis, pairs)  98.1 us
    dot_general x2, matrix products, line_transform(): sin_re = jnp.einsum('da,cak->cdk', line_sin, real_part, precision=PRECISE)  95.1 us
  transfers between devices with their start and end apart: 8, of which 8 were waited for; matrix products, arithmetic and copies ran while one was open for 12% of the time, Pallas kernels for 0%

commit v1 on v0

v1 whole, which is shorter than its diff:
```python
import functools
import math

import jax
import jax.numpy as jnp
import numpy as np
from jax import lax
from jax.experimental import pallas as pl
from jax.experimental.pallas import tpu as pltpu
from jax.sharding import PartitionSpec as P

HD = 128
MINOR = 128
ROWS = 256
BIG = -1e30


def hi_lo(x):
    high = x.astype(jnp.bfloat16)
    return high, (x - high.astype(jnp.float32)).astype(jnp.bfloat16)


def split_table(table):
    high = table.astype(jnp.bfloat16)
    low = (table - high.astype(np.float64)).astype(jnp.bfloat16)
    return jnp.asarray(np.stack([high, low]))


def dot3(table_ref, x):
    high, low = hi_lo(x)
    total = jnp.dot(table_ref[0], high, preferred_element_type=jnp.float32)
    total += jnp.dot(table_ref[0], low, preferred_element_type=jnp.float32)
    return total + jnp.dot(table_ref[1], high, preferred_element_type=jnp.float32)


def class_kernel(fwd_ref, inv_ref, twist_ref, sr_ref, si_ref, kr_ref, ki_ref, out_re, out_im):
    for n in range(sr_ref.shape[0]):
        cos = twist_ref[n, :, 0:1]
        sin = twist_ref[n, :, 1:2]

        def spectrum(re, im):
            turned = jnp.concatenate([re * cos + im * sin, im * cos - re * sin], axis=0)
            return dot3(fwd_ref, turned)

        sig = spectrum(sr_ref[n], si_ref[n])
        ker = spectrum(kr_ref[n], ki_ref[n])
        s_re, s_im, k_re, k_im = sig[:MINOR], sig[MINOR:], ker[:MINOR], ker[MINOR:]
        prod = jnp.concatenate([s_re * k_re - s_im * k_im, s_re * k_im + s_im * k_re], axis=0)
        back = dot3(inv_ref, prod)
        b_re, b_im = back[:MINOR], back[MINOR:]
        out_re[n] = b_re * cos - b_im * sin
        out_im[n] = b_im * cos + b_re * sin


def spectra_product(sig, ker, span):
    classes, _, chans = sig[0].shape
    step = max(d for d in range(1, 6) if classes % d == 0)
    index = np.arange(MINOR)
    angle = 2 * math.pi / MINOR * (np.outer(index, index) % MINOR)
    cos, sin = np.cos(angle), np.sin(angle)
    fwd = split_table(np.block([[cos, sin], [-sin, cos]]))
    inv = split_table(np.block([[cos, -sin], [sin, cos]]))
    turn = 2 * math.pi / span * np.outer(np.arange(classes), index)
    twist = jnp.asarray(np.stack([np.cos(turn), np.sin(turn)], axis=-1), jnp.float32)
    table = pl.BlockSpec((2, 2 * MINOR, 2 * MINOR), lambda i: (0, 0, 0))
    block = pl.BlockSpec((step, MINOR, chans), lambda i: (i, 0, 0))
    shape = jax.ShapeDtypeStruct((classes, MINOR, chans), jnp.float32)
    return pl.pallas_call(
        class_kernel,
        grid=(classes // step,),
        in_specs=[table, table, pl.BlockSpec((step, MINOR, 2), lambda i: (i, 0, 0))] + [block] * 4,
        out_specs=[block, block],
        out_shape=[shape, shape],
        compiler_params=pltpu.CompilerParams(vmem_limit_bytes=40 * 1024 * 1024),
        cost_estimate=pl.CostEstimate(
            flops=classes * 18 * 4 * MINOR * MINOR * chans,
            bytes_accessed=classes * MINOR * chans * 24,
            transcendentals=0,
        ),
        name="class_products",
    )(fwd, inv, twist, *sig, *ker)


def line_tables(lines):
    classes = lines // 2 + 1
    angle = 2 * math.pi / lines * (np.outer(np.arange(classes), np.arange(lines // 2)) % lines)
    return np.cos(angle), np.sin(angle)


def spread(blocks):
    cos, sin = line_tables(2 * blocks.shape[0])
    wave = jnp.asarray(np.stack([cos, -sin]), jnp.float32)
    out = jnp.einsum(
        "rpk,kqc->rpqc", wave, blocks.astype(jnp.float32), precision=lax.Precision.HIGH
    )
    return out[0], out[1]


def gather_lines(re, im, lines):
    cos, sin = line_tables(lines)
    weight = np.full((lines // 2 + 1, 1), 2.0)
    weight[0] = weight[-1] = 1.0
    weight /= lines * MINOR
    cos = jnp.asarray((weight * cos).T, jnp.float32)
    sin = jnp.asarray((weight * sin).T, jnp.float32)
    out = jnp.einsum("tp,pqc->tqc", cos, re, precision=lax.Precision.HIGH)
    return out - jnp.einsum("tp,pqc->tqc", sin, im, precision=lax.Precision.HIGH)


def to_channels(x, devices):
    rows, chans = x.shape
    each = chans // devices
    pieces = x.reshape(rows, devices, each).transpose(1, 0, 2)
    got = lax.all_to_all(pieces, "seq", split_axis=0, concat_axis=0, tiled=True)
    return got.reshape(devices * rows // MINOR, MINOR, each)


def to_rows(x, devices):
    lines, _, each = x.shape
    rows = lines * MINOR // devices
    got = lax.all_to_all(
        x.reshape(devices, rows, each), "seq", split_axis=0, concat_axis=0, tiled=True
    )
    return got.transpose(1, 0, 2).reshape(rows, devices * each)


def attend_kernel(groups, bias_ref, q_ref, k_ref, v_ref, out_ref, lse_ref):
    tokens = k_ref.shape[0] // 2
    tile = ROWS // groups
    scale = HD ** (-0.5)
    rate = scale * math.log2(math.e)
    bias = bias_ref[0, 0]
    v_turned = v_ref[...].T
    key_row = lax.broadcasted_iota(jnp.int32, (tile, ROWS), 0)
    query_row = lax.broadcasted_iota(jnp.int32, (tile, ROWS), 1) // groups
    allowed = key_row <= query_row
    for i in range(tokens // tile):
        rows = slice(i * ROWS, (i + 1) * ROWS)
        keys = tokens + (i + 1) * tile
        scores = lax.dot_general(
            k_ref[:keys, :],
            q_ref[rows, :],
            (((1,), (1,)), ((), ())),
            preferred_element_type=jnp.float32,
        )
        pieces = [scores[:tokens] + bias]
        if i:
            pieces.append(scores[tokens : keys - tile])
        pieces.append(jnp.where(allowed, scores[keys - tile :], BIG))
        scores = jnp.concatenate(pieces, axis=0)
        peak = jnp.max(scores, axis=0, keepdims=True)
        weights = jnp.exp2((scores - peak) * rate)
        total = jnp.sum(weights, axis=0, keepdims=True)
        mixed = jnp.dot(
            v_turned[:, :keys],
            weights.astype(jnp.bfloat16),
            preferred_element_type=jnp.float32,
        )
        out_ref[rows, :] = (mixed * (1.0 / total)).T.astype(jnp.bfloat16)
        lse_ref[0, :, rows] = peak * scale + jnp.log(total)


def attend(attn_query, keys, values, my_index):
    tokens, groups, features = attn_query.shape
    heads = features // HD
    rows = tokens * groups
    bias = jnp.where(my_index > 0, 0.0, BIG).astype(jnp.float32).reshape(1, 1)
    column = lambda n: pl.BlockSpec((n, HD), lambda j: (0, j))
    out, lse = pl.pallas_call(
        functools.partial(attend_kernel, groups),
        grid=(heads,),
        in_specs=[
            pl.BlockSpec((1, 1), lambda j: (0, 0), memory_space=pltpu.SMEM),
            column(rows),
            column(2 * tokens),
            column(2 * tokens),
        ],
        out_specs=[column(rows), pl.BlockSpec((1, 1, rows), lambda j: (j, 0, 0))],
        out_shape=[
            jax.ShapeDtypeStruct((rows, features), jnp.bfloat16),
            jax.ShapeDtypeStruct((heads, 1, rows), jnp.float32),
        ],
        compiler_params=pltpu.CompilerParams(vmem_limit_bytes=40 * 1024 * 1024),
        cost_estimate=pl.CostEstimate(
            flops=heads * rows * 2 * tokens * HD * 4,
            bytes_accessed=rows * features * 4 + tokens * features * 8,
            transcendentals=heads * rows * 2 * tokens,
        ),
        name="attend",
    )(bias, attn_query.reshape(rows, features), keys, values)
    lse = lse.reshape(heads, tokens, groups).transpose(2, 0, 1)
    return out.reshape(tokens, groups, features), lse


def local(
    hyena_gate, hyena_key, hyena_value, long_filter, skip_weight, attn_query, attn_keys, attn_values
):
    devices = lax.axis_size("seq")
    my_index = lax.axis_index("seq")
    kv_pair = jnp.stack([attn_keys, attn_values])
    behind = lax.ppermute(kv_pair, "seq", [(i, i + 1) for i in range(devices - 1)])
    ker_blocks = to_channels(long_filter, devices)
    signal = hyena_key.astype(jnp.float32) * hyena_value.astype(jnp.float32)
    sig_blocks = to_channels(signal.astype(jnp.bfloat16), devices)
    window = jnp.concatenate([behind, kv_pair], axis=1)
    window = lax.all_gather(window, "chan", axis=2, tiled=True)
    attn_out, attn_lse = attend(attn_query, window[0], window[1], my_index)
    lines = 2 * ker_blocks.shape[0]
    ker = spread(ker_blocks)
    sig = spread(sig_blocks)
    back = spectra_product(sig, ker, lines * MINOR)
    conv = to_rows(gather_lines(*back, lines).astype(jnp.bfloat16), devices)
    signal = hyena_key.astype(jnp.float32) * hyena_value.astype(jnp.float32)
    hyena_out = hyena_gate.astype(jnp.float32) * (
        conv.astype(jnp.float32) + skip_weight * signal
    )
    return (hyena_out.astype(jnp.bfloat16), attn_out, attn_lse)


def solution(mesh):
    return jax.shard_map(
        local,
        mesh=mesh,
        in_specs=(
            P("seq", "chan"),
            P("seq", "chan"),
            P("seq", "chan"),
            P("seq", "chan"),
            P("chan"),
            P("seq", "chan", None),
            P("seq", "chan"),
            P("seq", "chan"),
        ),
        out_specs=(P("seq", "chan"), P("seq", "chan", None), P("chan", None, "seq")),
        check_vma=False,
    )
```

time: 2050 us -> 335 us (0.16)
  waiting for transfers between devices: 1160 us -> 91.2 us
  matrix products: 508 us -> 18.8 us
  local copies, waits for them, and re-layouts: 173 us -> 78.3 us
  starting transfers between devices: 127 us -> 38.3 us
  Pallas kernels: 0 us -> 77.9 us
  other arithmetic: 58.7 us -> 14.2 us
    all_to_all x6 -> x3, waiting for transfers between devices: 1040 us -> 44.2 us  [the longest x2 44.2 us: to_channels(): got = lax.all_to_all(pieces, 'seq', split_axis=0, concat_axis=0, tiled=True)]
    dot_general x14 -> x4, matrix products: 508 us -> 18.8 us  [the longest x2 9.36 us: spread(): jnp.einsum('rpk,kqc->rpqc', wave, blocks.astype(jnp.float32), precision=l...]
    all_to_all x6 -> x3, starting transfers between devices: 123 us -> 34.7 us  [the longest x1 22.6 us: to_rows(): lax.all_to_all(x.reshape(devices, rows, each), 'seq', split_axis=0, conca...]
    pallas_call x0 -> x2, Pallas kernels: none -> 77.9 us  [the longest x1 40.6 us: attend(): pl.pallas_call(functools.partial(attend_kernel, groups), grid=(heads,), i...]
    all_to_all x8 -> x2, local copies, waits for them, and re-layouts: 69.2 us -> 7.82 us  [to_channels(): got = lax.all_to_all(pieces, 'seq', split_axis=0, concat_axis=0, tiled=True)]
    ppermute x1, waiting for transfers between devices: 98.1 us -> 47 us  [local(): lax.ppermute(kv_pair, 'seq', [(i, i + 1) for i in range(devices - 1)])]
    add x2 -> x0, local copies, waits for them, and re-layouts: 31.4 us -> none  [the longest x1 18 us: long_conv(): turned_re = spread_re * twist_cos + spread_im * twist_sin]
    sub x2 -> x0, local copies, waits for them, and re-layouts: 31.1 us -> none  [the longest x1 17.7 us: long_conv(): turned_im = spread_im * twist_cos - spread_re * twist_sin]
  transfers between devices with their start and end apart: 8 -> 5, of which waited for: 8 -> 2; matrix products, arithmetic and copies ran while one was open for 12% -> 24% of each run, Pallas kernels for 0% -> 23%
where the time goes in v1:
time: 335 us; the launch traced here: 333 us
  waiting for transfers between devices  91.2 us (27%)
  local copies, waits for them, and re-layouts  78.3 us (23%)
  Pallas kernels  77.9 us (23%)
  starting transfers between devices  38.3 us (11%)
  matrix products  18.8 us (6%)
  between operations  14.3 us (4%)
  other arithmetic  14.2 us (4%)
    ppermute x1, waiting for transfers between devices, local(): lax.ppermute(kv_pair, 'seq', [(i, i + 1) for i in range(devices - 1)])  47 us
    all_to_all x2, waiting for transfers between devices, to_channels(): got = lax.all_to_all(pieces, 'seq', split_axis=0, concat_axis=0, tiled=True)  44.2 us
    pallas_call x1, Pallas kernels, attend(): pl.pallas_call(functools.partial(attend_kernel, groups), grid=(heads,), i...  40.6 us
    pallas_call x1, Pallas kernels, spectra_product(): pl.pallas_call(class_kernel, grid=(classes // step,), in_specs=[table, ta...  37.3 us
    all_to_all x1, starting transfers between devices, to_rows(): lax.all_to_all(x.reshape(devices, rows, each), 'seq', split_axis=0, conca...  22.6 us
    unnamed x38, local copies, waits for them, and re-layouts  22.3 us
    squeeze x2, local copies, waits for them, and re-layouts, spread(): return (out[0], out[1])  14 us
    all_to_all x2, starting transfers between devices, to_channels(): got = lax.all_to_all(pieces, 'seq', split_axis=0, concat_axis=0, tiled=True)  12.1 us
  transfers between devices with their start and end apart: 5, of which 2 were waited for; matrix products, arithmetic and copies ran while one was open for 24% of the time, Pallas kernels for 23%

profile of v1, /device:TPU:12, one launch (start us, length us, event | category | flops | bytes accessed | tf_op | source)
XLA Modules:
  0.0 333.0 jit_solution(12826599592662301846)
XLA Ops:
  7.2 2.9 copy.37
  10.0 3.9 %copy.38 = bf16[512,2048]{0,1:T(8,128)(2,1)} copy(bf16[512,2048]{1,0:T(8,128)(2,1)} %param.17) | data formatting | bytes 4194304 | tf_op args[2]
  14.0 3.5 %fusion.6 = bf16[512,2048]{0,1:T(8,128)(2,1)} fusion(bf16[512,2048]{0,1:T(8,128)(2,1)} %copy.38, bf16[512,2048]{0,1:T(8,128)(2,1)S(1)} %copy.37), kind=kLoop, calls=%fused_computation.14 | loop fusion | flops 4194304 | bytes 6291456 | tf_op jit(solution)/shard_map/convert_element_type | solution.py:204
  17.5 7.2 %all-to-all-start = ((bf16[16,512,128]{1,2,0:T(8,128)(2,1)}), bf16[16,512,128]{1,2,0:T(8,128)(2,1)}, u32[]{:S(2)}, u32[]{:S(2)}) async-start(bf16[16,512,128]{1,2,0:T(8,128)(2,1)} %bitcast.56), calls=%async_computation | async-start | bytes 4194304 | tf_op jit(solution)/shard_map/all_to_all | solution.py:114
  24.7 4.0 %copy.43 = bf16[512,2048]{0,1:T(8,128)(2,1)} copy(bf16[512,2048]{1,0:T(8,128)(2,1)} %param.18) | data formatting | bytes 4194304 | tf_op args[3]
  28.7 44.2 %all-to-all-done = bf16[16,512,128]{1,2,0:T(8,128)(2,1)} async-done(((bf16[16,512,128]{1,2,0:T(8,128)(2,1)}), bf16[16,512,128]{1,2,0:T(8,128)(2,1)}, u32[]{:S(2)}, u32[]{:S(2)}) %all-to-all-start) | async-done | bytes 2097184 | tf_op jit(solution)/shard_map/all_to_all | solution.py:114
  72.9 4.9 %all-to-all-start.1 = ((bf16[16,512,128]{1,2,0:T(8,128)(2,1)}), bf16[16,512,128]{1,2,0:T(8,128)(2,1)}, u32[]{:S(2)}, u32[]{:S(2)}) async-start(bf16[16,512,128]{1,2,0:T(8,128)(2,1)} %bitcast.58), calls=%async_computation.1 | async-start | bytes 4194304 | tf_op jit(solution)/shard_map/all_to_all | solution.py:114
  78.0 3.6 %collective-permute-start = (bf16[2,512,512]{2,1,0:T(8,128)(2,1)S(1)}, bf16[2,512,512]{2,1,0:T(8,128)(2,1)S(1)}, u32[]{:S(2)}, u32[]{:S(2)}) collective-permute-start(bf16[2,512,512]{2,1,0:T(8,128)(2,1)S(1)} %pad_maximum_fusion), channel_id=1, source_target_pairs={{0,2},{2,4},{4,6},{6,8},{8,10},{10,12},{12,14},{14,16},{16,18},{18... | collective-permute-start | bytes 3145736 | tf_op jit(solution)/shard_map/ppermute | solution.py:201
  81.5 47.0 %collective-permute-done = bf16[2,512,512]{2,1,0:T(8,128)(2,1)S(1)} collective-permute-done((bf16[2,512,512]{2,1,0:T(8,128)(2,1)S(1)}, bf16[2,512,512]{2,1,0:T(8,128)(2,1)S(1)}, u32[]{:S(2)}, u32[]{:S(2)}) %collective-permute-start) | collective-permute-done | bytes 1048608 | tf_op jit(solution)/shard_map/ppermute | solution.py:201
  130.1 3.9 %copy.39 = bf16[16,512,128]{2,1,0:T(8,128)(2,1)} copy(bf16[16,512,128]{1,2,0:T(8,128)(2,1)} %all-to-all-done) | data formatting | bytes 4194304 | tf_op jit(solution)/shard_map/all_to_all | solution.py:114
  134.0 4.6 %fusion.11 = f32[2,65,128,128]{3,1,2,0:T(8,128)S(1)} fusion(f32[2,65,64,1]{1,2,3,0:T(8,128)S(1)} %copy-done.8, bf16[64,128,128]{2,1,0:T(8,128)(2,1)} %bitcast.60), kind=kOutput, calls=%fused_computation.20 | convolution fusion | flops 817889280 | bytes 10650112 | tf_op jit(solution)/shard_map/rpk,kqc->rpqc/dot_general | solution.py:93
  138.6 4.3 %fusion.19 = (f32[1,65,128,128]{3,1,2,0:T(8,128)}, f32[1,65,128,128]{3,1,2,0:T(8,128)}) fusion(f32[2,65,128,128]{3,1,2,0:T(8,128)S(1)} %fusion.11), kind=kLoop, calls=%fused_computation.27 | loop fusion | bytes 17039360 | tf_op jit(solution)/shard_map/slice | solution.py:96
  142.9 3.9 %copy.44 = bf16[16,512,128]{2,1,0:T(8,128)(2,1)} copy(bf16[16,512,128]{1,2,0:T(8,128)(2,1)} %all-to-all-done.1) | data formatting | bytes 4194304 | tf_op jit(solution)/shard_map/all_to_all | solution.py:114
  146.8 4.8 %fusion.9 = f32[2,65,128,128]{3,1,2,0:T(8,128)S(1)} fusion(f32[2,65,64,1]{1,2,3,0:T(8,128)S(1)} %copy-done.8, bf16[64,128,128]{2,1,0:T(8,128)(2,1)} %bitcast.59), kind=kOutput, calls=%fused_computation.18 | convolution fusion | flops 817889280 | bytes 10650112 | tf_op jit(solution)/shard_map/rpk,kqc->rpqc/dot_general | solution.py:93
  151.6 4.7 %fusion.18 = (f32[1,65,128,128]{3,1,2,0:T(8,128)}, f32[1,65,128,128]{3,1,2,0:T(8,128)}) fusion(f32[2,65,128,128]{3,1,2,0:T(8,128)S(1)} %fusion.9), kind=kLoop, calls=%fused_computation.26 | loop fusion | bytes 17039360 | tf_op jit(solution)/shard_map/slice | solution.py:96
  156.3 8.9 %copy_bitcast_fusion.2 = (f32[65,128,128]{2,1,0:T(8,128)}, f32[65,128,128]{2,1,0:T(8,128)}) fusion(f32[1,65,128,128]{3,1,2,0:T(8,128)S(1)} %bitcast.55, f32[1,65,128,128]{3,1,2,0:T(8,128)} %get-tuple-element.20), kind=kLoop, calls=%fused_computation.6 | loop fusion | bytes 17039360 | tf_op jit(solution)/shard_map/squeeze | solution.py:96
  165.2 5.1 %copy_bitcast_fusion = (f32[65,128,128]{2,1,0:T(8,128)}, f32[65,128,128]{2,1,0:T(8,128)}) fusion(f32[1,65,128,128]{3,1,2,0:T(8,128)S(1)} %copy-done.4, f32[1,65,128,128]{3,1,2,0:T(8,128)S(1)} %copy-done.5), kind=kLoop, calls=%fused_computation.4 | loop fusion | bytes 17039360 | tf_op jit(solution)/shard_map/squeeze | solution.py:96
  170.4 37.3 %class_products.1 = (f32[65,128,128]{2,1,0:T(8,128)S(1)}, f32[65,128,128]{2,1,0:T(8,128)S(1)}) custom-call(bf16[2,256,256]{2,1,0:T(8,128)(2,1)S(1)} %copy-done.2, bf16[2,256,256]{2,1,0:T(8,128)(2,1)S(1)} %copy-done.3, f32[65,128,2]{2,1,0:T(8,128)S(1)} %bitcast.53, f32[65,128,128]{2,1,0:T(8,128)} %get-tuple-element.24.sr_ref, ...), custom_call_target="tpu_custom_call" | custom-call | flops 9814671360 | bytes 25559040 | tf_op jit(solution)/shard_map/class_products/pallas_call | solution.py:68
  207.7 4.5 %fusion = f32[128,128,64]{1,2,0:T(8,128)S(1)} fusion(f32[64,65,1]{1,0,2:T(8,128)S(1)} %copy-done.10, f32[65,128,128]{2,1,0:T(8,128)S(1)} %get-tuple-element.8), kind=kOutput, calls=%fused_computation | convolution fusion | flops 408944640 | bytes 8470784 | tf_op jit(solution)/shard_map/tp,pqc->tqc/dot_general | solution.py:107
  212.2 5.0 %fusion.15 = bf16[64,128,128]{2,0,1:T(8,128)(2,1)S(1)} fusion(f32[128,128,64]{1,2,0:T(8,128)S(1)} %fusion, f32[64,65,1]{1,0,2:T(8,128)S(1)} %copy-done.9, f32[65,128,128]{2,1,0:T(8,128)S(1)} %get-tuple-element.7), kind=kOutput, calls=%fused_computation.24 | convolution fusion | flops 411041792 | bytes 10567936 | tf_op jit(solution)/shard_map/tp,pqc->tqc/dot_general | solution.py:106
  217.2 2.7 copy.50
  219.9 22.6 %all-to-all-start.2 = ((bf16[16,512,128]{2,1,0:T(8,128)(2,1)}), bf16[16,512,128]{2,1,0:T(8,128)(2,1)}, u32[]{:S(2)}, u32[]{:S(2)}) async-start(bf16[16,512,128]{2,1,0:T(8,128)(2,1)} %bitcast.57), calls=%async_computation.2 | async-start | bytes 4194304 | tf_op jit(solution)/shard_map/all_to_all | solution.py:121
  242.5 4.0 %copy.36 = bf16[512,2048]{0,1:T(8,128)(2,1)} copy(bf16[512,2048]{1,0:T(8,128)(2,1)} %param.15) | data formatting | bytes 4194304 | tf_op args[0]
  246.5 6.9 %reshape.43.q_ref = bf16[2048,1024]{1,0:T(8,128)(2,1)} reshape(bf16[512,4,1024]{2,1,0:T(4,128)(2,1)} %param.20) | data formatting | bytes 8388608 | tf_op jit(solution)/shard_map/reshape | solution.py:190
  253.4 2.8 slice_bitcast_fusion
  256.8 40.6 %attend.1 = (bf16[2048,1024]{1,0:T(8,128)(2,1)S(1)}, f32[8,1,2048]{2,1,0:T(1,128)S(1)}) custom-call(f32[1,1]{1,0:T(1,128)} %bitcast.21.bias_ref, bf16[2048,1024]{1,0:T(8,128)(2,1)S(1)} %copy-done, bf16[1024,1024]{1,0:T(8,128)(2,1)S(1)} %get-tuple-element.22.k_ref, bf16[1024,1024]{1,0:T(8,128)(2,1)S(1)} %get-tuple-element.21.v_ref), custom_call_target="tpu_custom_call" | custom-call | flops 8589934592 | bytes 12582912 | tf_op jit(solution)/shard_map/attend/pallas_call | solution.py:169
  297.4 2.0 copy-done.1
  299.4 7.2 %reshape.44 = bf16[512,4,1024]{2,1,0:T(4,128)(2,1)} reshape(bf16[2048,1024]{1,0:T(8,128)(2,1)} %copy-done.1) | data formatting | bytes 8388608 | tf_op jit(solution)/shard_map/reshape | solution.py:192
  307.8 4.1 %convert_bitcast_fusion = f32[512,16,128]{2,0,1:T(8,128)} fusion(bf16[16,512,128]{2,1,0:T(8,128)(2,1)} %all-to-all-done.2), kind=kLoop, calls=%fused_computation.11 | loop fusion | flops 1048576 | bytes 6291456 | tf_op jit(solution)/shard_map/convert_element_type | solution.py:215
  311.9 5.4 %copy.51 = f32[512,16,128]{0,2,1:T(8,128)} copy(f32[512,16,128]{2,0,1:T(8,128)} %convert_bitcast_fusion) | data formatting | bytes 8388608 | tf_op jit(solution)/shard_map/convert_element_type | solution.py:215
  317.3 5.0 %fusion.5 = bf16[512,2048]{0,1:T(8,128)(2,1)} fusion(f32[512,16,128]{0,2,1:T(8,128)} %copy.51, bf16[512,2048]{0,1:T(8,128)(2,1)} %copy.36, bf16[512,2048]{0,1:T(8,128)(2,1)} %copy.38, bf16[512,2048]{0,1:T(8,128)(2,1)S(1)} %copy.37, f32[2048]{0:T(1024)S(1)} %copy-done.11), kind=kLoop, calls=%fused_computation.10 | loop fusion | flops 8388608 | bytes 12591104 | tf_op jit(solution)/shard_map/convert_element_type | solution.py:217
  322.3 3.9 %copy.53 = bf16[512,2048]{1,0:T(8,128)(2,1)} copy(bf16[512,2048]{0,1:T(8,128)(2,1)} %fusion.5) | data formatting | bytes 4194304
  (42 shorter events, 3.7 us)
Async XLA Ops:
  17.5 55.4 %all-to-all-start = ((bf16[16,512,128]{1,2,0:T(8,128)(2,1)}), bf16[16,512,128]{1,2,0:T(8,128)(2,1)}, u32[]{:S(2)}, u32[]{:S(2)}) async-start(bf16[16,512,128]{1,2,0:T(8,128)(2,1)} %bitcast.56), calls=%async_computation | async-start | bytes 4194304 | tf_op jit(solution)/shard_map/all_to_all | solution.py:114
  24.6 53.2 %copy-start.6 = (bf16[512,512]{1,0:T(8,128)(2,1)S(1)}, bf16[512,512]{1,0:T(8,128)(2,1)}, u32[]{:S(2)}) copy-start(bf16[512,512]{1,0:T(8,128)(2,1)} %param.22) | copy-start | bytes 1572868
  24.6 53.2 %copy-start.7 = (bf16[512,512]{1,0:T(8,128)(2,1)S(1)}, bf16[512,512]{1,0:T(8,128)(2,1)}, u32[]{:S(2)}) copy-start(bf16[512,512]{1,0:T(8,128)(2,1)} %param.21) | copy-start | bytes 1572868
  72.9 70.0 %all-to-all-start.1 = ((bf16[16,512,128]{1,2,0:T(8,128)(2,1)}), bf16[16,512,128]{1,2,0:T(8,128)(2,1)}, u32[]{:S(2)}, u32[]{:S(2)}) async-start(bf16[16,512,128]{1,2,0:T(8,128)(2,1)} %bitcast.58), calls=%async_computation.1 | async-start | bytes 4194304 | tf_op jit(solution)/shard_map/all_to_all | solution.py:114
  77.8 175.6 %all-gather.2.cloned.1.call-start = ((), (), s32[]{:S(2)}) async-start(), calls=%async_computation.3 | async-start | bytes 6291456 | tf_op jit(solution)/shard_map/all_gather | solution.py:206
  78.0 50.6 %collective-permute-start = (bf16[2,512,512]{2,1,0:T(8,128)(2,1)S(1)}, bf16[2,512,512]{2,1,0:T(8,128)(2,1)S(1)}, u32[]{:S(2)}, u32[]{:S(2)}) collective-permute-start(bf16[2,512,512]{2,1,0:T(8,128)(2,1)S(1)} %pad_maximum_fusion), channel_id=1, source_target_pairs={{0,2},{2,4},{4,6},{6,8},{8,10},{10,12},{12,14},{14,16},{16,18},{18... | collective-permute-start | bytes 3145736 | tf_op jit(solution)/shard_map/ppermute | solution.py:201
  130.1 3.9 %copy-start.8 = (f32[2,65,64,1]{1,2,3,0:T(8,128)S(1)}, f32[2,65,64,1]{1,2,3,0:T(8,128)}, u32[]{:S(2)}) copy-start(f32[2,65,64,1]{1,2,3,0:T(8,128)} %constant.30) | copy-start | bytes 99844
  146.8 9.5 %slice-start.2 = ((s8[4718592]{0:T(1024)(128)(4,1)}), s8[4194304]{0:T(1024)(128)(4,1)S(1)}, s32[]{:S(2)}) async-start(s8[4718592]{0:T(1024)(128)(4,1)} %bitcast.54), calls=%async_computation.6 | async-start | bytes 8388608
  151.6 4.7 %slice-start.3 = ((s8[4718592]{0:T(1024)(128)(4,1)}), s8[524288]{0:T(1024)(128)(4,1)S(1)}, s32[]{:S(2)}) async-start(s8[4718592]{0:T(1024)(128)(4,1)} %bitcast.54), calls=%async_computation.7 | async-start | bytes 1048576
  156.3 9.0 %copy-start.4 = (f32[1,65,128,128]{3,1,2,0:T(8,128)S(1)}, f32[1,65,128,128]{3,1,2,0:T(8,128)}, u32[]{:S(2)}) copy-start(f32[1,65,128,128]{3,1,2,0:T(8,128)} %get-tuple-element.17) | copy-start | bytes 12779524
  156.3 8.9 %copy-start.5 = (f32[1,65,128,128]{3,1,2,0:T(8,128)S(1)}, f32[1,65,128,128]{3,1,2,0:T(8,128)}, u32[]{:S(2)}) copy-start(f32[1,65,128,128]{3,1,2,0:T(8,128)} %get-tuple-element.18) | copy-start | bytes 12779524
  156.3 14.0 %slice-start = ((s8[4259840]{0:T(1024)(128)(4,1)}), s8[4194304]{0:T(1024)(128)(4,1)S(1)}, s32[]{:S(2)}) async-start(s8[4259840]{0:T(1024)(128)(4,1)} %bitcast.52), calls=%async_computation.4 | async-start | bytes 8388608
  165.2 5.1 %slice-start.1 = ((s8[4259840]{0:T(1024)(128)(4,1)}), s8[65536]{0:T(1024)(128)(4,1)S(1)}, s32[]{:S(2)}) async-start(s8[4259840]{0:T(1024)(128)(4,1)} %bitcast.52), calls=%async_computation.5 | async-start | bytes 131072
  165.2 5.1 %copy-start.2 = (bf16[2,256,256]{2,1,0:T(8,128)(2,1)S(1)}, bf16[2,256,256]{2,1,0:T(8,128)(2,1)}, u32[]{:S(2)}) copy-start(bf16[2,256,256]{2,1,0:T(8,128)(2,1)} %constant.25.clone.fwd_ref) | copy-start | bytes 786436
  165.2 5.1 %copy-start.3 = (bf16[2,256,256]{2,1,0:T(8,128)(2,1)S(1)}, bf16[2,256,256]{2,1,0:T(8,128)(2,1)}, u32[]{:S(2)}) copy-start(bf16[2,256,256]{2,1,0:T(8,128)(2,1)} %constant.26.clone.inv_ref) | copy-start | bytes 786436
  170.3 37.3 %copy-start.10 = (f32[64,65,1]{1,0,2:T(8,128)S(1)}, f32[64,65,1]{1,0,2:T(8,128)}, u32[]{:S(2)}) copy-start(f32[64,65,1]{1,0,2:T(8,128)} %constant.32) | copy-start | bytes 49924
  207.7 4.5 %copy-start.9 = (f32[64,65,1]{1,0,2:T(8,128)S(1)}, f32[64,65,1]{1,0,2:T(8,128)}, u32[]{:S(2)}) copy-start(f32[64,65,1]{1,0,2:T(8,128)} %constant.31) | copy-start | bytes 49924
  219.9 88.0 %all-to-all-start.2 = ((bf16[16,512,128]{2,1,0:T(8,128)(2,1)}), bf16[16,512,128]{2,1,0:T(8,128)(2,1)}, u32[]{:S(2)}, u32[]{:S(2)}) async-start(bf16[16,512,128]{2,1,0:T(8,128)(2,1)} %bitcast.57), calls=%async_computation.2 | async-start | bytes 4194304 | tf_op jit(solution)/shard_map/all_to_all | solution.py:121
  253.4 3.4 %copy-start = (bf16[2048,1024]{1,0:T(8,128)(2,1)S(1)}, bf16[2048,1024]{1,0:T(8,128)(2,1)}, u32[]{:S(2)}) copy-start(bf16[2048,1024]{1,0:T(8,128)(2,1)} %reshape.43.q_ref) | copy-start | bytes 12582916
  297.4 2.0 copy-start.1
  311.9 5.4 %copy-start.11 = (f32[2048]{0:T(1024)S(1)}, f32[2048]{0:T(1024)}, u32[]{:S(2)}) copy-start(f32[2048]{0:T(1024)} %param.19) | copy-start | bytes 24580
Sparse Core Ops, SparseCore 0:
  130.2 31.3 all-gather.1

commit v2 on v1

--- a/solution.py
+++ b/solution.py
@@ -107,75 +107,63 @@
     return out - jnp.einsum("tp,pqc->tqc", sin, im, precision=lax.Precision.HIGH)
 
 
-def to_channels(x, devices):
-    rows, chans = x.shape
-    each = chans // devices
-    pieces = x.reshape(rows, devices, each).transpose(1, 0, 2)
-    got = lax.all_to_all(pieces, "seq", split_axis=0, concat_axis=0, tiled=True)
-    return got.reshape(devices * rows // MINOR, MINOR, each)
-
-
-def to_rows(x, devices):
-    lines, _, each = x.shape
-    rows = lines * MINOR // devices
-    got = lax.all_to_all(
-        x.reshape(devices, rows, each), "seq", split_axis=0, concat_axis=0, tiled=True
-    )
-    return got.transpose(1, 0, 2).reshape(rows, devices * each)
-
-
-def attend_kernel(groups, bias_ref, q_ref, k_ref, v_ref, out_ref, lse_ref):
-    tokens = k_ref.shape[0] // 2
+def attend_kernel(groups, bias_ref, q_ref, kp_ref, vp_ref, ko_ref, vo_ref, out_ref, lse_ref):
+    tokens = ko_ref.shape[1]
     tile = ROWS // groups
     scale = HD ** (-0.5)
     rate = scale * math.log2(math.e)
     bias = bias_ref[0, 0]
-    v_turned = v_ref[...].T
+    v_before = vp_ref[0].T
+    v_own = vo_ref[0].T
     key_row = lax.broadcasted_iota(jnp.int32, (tile, ROWS), 0)
     query_row = lax.broadcasted_iota(jnp.int32, (tile, ROWS), 1) // groups
     allowed = key_row <= query_row
+    contract = functools.partial(
+        lax.dot_general,
+        dimension_numbers=(((1,), (1,)), ((), ())),
+        preferred_element_type=jnp.float32,
+    )
     for i in range(tokens // tile):
         rows = slice(i * ROWS, (i + 1) * ROWS)
-        keys = tokens + (i + 1) * tile
-        scores = lax.dot_general(
-            k_ref[:keys, :],
-            q_ref[rows, :],
-            (((1,), (1,)), ((), ())),
-            preferred_element_type=jnp.float32,
-        )
-        pieces = [scores[:tokens] + bias]
-        if i:
-            pieces.append(scores[tokens : keys - tile])
-        pieces.append(jnp.where(allowed, scores[keys - tile :], BIG))
-        scores = jnp.concatenate(pieces, axis=0)
-        peak = jnp.max(scores, axis=0, keepdims=True)
-        weights = jnp.exp2((scores - peak) * rate)
-        total = jnp.sum(weights, axis=0, keepdims=True)
+        keys = (i + 1) * tile
+        query = q_ref[rows, :]
+        before = contract(kp_ref[0], query) + bias
+        own = contract(ko_ref[0, :keys, :], query)
+        last = jnp.where(allowed, own[keys - tile :], BIG)
+        own = jnp.concatenate([own[: keys - tile], last], axis=0) if i else last
+        peak = jnp.maximum(
+            jnp.max(before, axis=0, keepdims=True), jnp.max(own, axis=0, keepdims=True)
+        )
+        before = jnp.exp2((before - peak) * rate)
+        own = jnp.exp2((own - peak) * rate)
+        total = jnp.sum(before, axis=0, keepdims=True) + jnp.sum(own, axis=0, keepdims=True)
         mixed = jnp.dot(
-            v_turned[:, :keys],
-            weights.astype(jnp.bfloat16),
-            preferred_element_type=jnp.float32,
-        )
+            v_before, before.astype(jnp.bfloat16), preferred_element_type=jnp.float32
+        ) + jnp.dot(v_own[:, :keys], own.astype(jnp.bfloat16), preferred_element_type=jnp.float32)
         out_ref[rows, :] = (mixed * (1.0 / total)).T.astype(jnp.bfloat16)
         lse_ref[0, :, rows] = peak * scale + jnp.log(total)
 
 
-def attend(attn_query, keys, values, my_index):
-    tokens, groups, features = attn_query.shape
+def attend(queries, groups, behind, own, my_index):
+    rows, features = queries.shape
+    tokens = rows // groups
     heads = features // HD
-    rows = tokens * groups
     bias = jnp.where(my_index > 0, 0.0, BIG).astype(jnp.float32).reshape(1, 1)
-    column = lambda n: pl.BlockSpec((n, HD), lambda j: (0, j))
-    out, lse = pl.pallas_call(
+    column = pl.BlockSpec((rows, HD), lambda j: (0, j))
+    keys = pl.BlockSpec((1, tokens, HD), lambda j: (0, 0, j))
+    values = pl.BlockSpec((1, tokens, HD), lambda j: (1, 0, j))
+    return pl.pallas_call(
         functools.partial(attend_kernel, groups),
         grid=(heads,),
         in_specs=[
             pl.BlockSpec((1, 1), lambda j: (0, 0), memory_space=pltpu.SMEM),
-            column(rows),
-            column(2 * tokens),
-            column(2 * tokens),
+            column,
+            keys,
+            values,
+            keys,
+            values,
         ],
-        out_specs=[column(rows), pl.BlockSpec((1, 1, rows), lambda j: (j, 0, 0))],
+        out_specs=[column, pl.BlockSpec((1, 1, rows), lambda j: (j, 0, 0))],
         out_shape=[
             jax.ShapeDtypeStruct((rows, features), jnp.bfloat16),
             jax.ShapeDtypeStruct((heads, 1, rows), jnp.float32),
@@ -187,9 +175,185 @@
             transcendentals=heads * rows * 2 * tokens,
         ),
         name="attend",
-    )(bias, attn_query.reshape(rows, features), keys, values)
-    lse = lse.reshape(heads, tokens, groups).transpose(2, 0, 1)
-    return out.reshape(tokens, groups, features), lse
+    )(bias, queries, behind, behind, own, own)
+
+
+def conv_kernel(w1_ref, w2_ref, fwd_ref, inv_ref, twist_ref, sig_ref, ker_ref, out_ref,
+                wide_ref, sig_lines, ker_lines):
+    half = sig_ref.shape[0] // MINOR
+    both = w1_ref.shape[0]
+    slots = both // 2
+    chans = sig_ref.shape[1]
+    piece = min(1024, sig_ref.shape[0])
+
+    for source, lines in ((sig_ref, sig_lines), (ker_ref, ker_lines)):
+
+        def widen(i, _):
+            at = pl.ds(pl.multiple_of(i * piece, piece), piece)
+            wide_ref[at, :] = source[at, :].astype(jnp.float32)
+            return 0
+
+        lax.fori_loop(0, source.shape[0] // piece, widen, 0)
+
+        def first(i, _):
+            cols = [wide_ref[pl.ds(2 * i + d, half, stride=MINOR), :] for d in range(2)]
+            col = jnp.concatenate(cols, axis=1).astype(jnp.bfloat16)
+            got = jnp.dot(
+                w1_ref[...],
+                jnp.concatenate([col, col], axis=0),
+                preferred_element_type=jnp.float32,
+            )
+            for d in range(2):
+                at = pl.ds(pl.multiple_of((2 * i + d) * both, 8), both)
+                lines[at, :] = got[:, d * chans : (d + 1) * chans]
+            return 0
+
+        lax.fori_loop(0, MINOR // 2, first, 0, unroll=2)
+
+    def pair(i, _):
+        prods, turns = [], []
+        for d in range(2):
+            n = 2 * i + d
+            at_re = pl.ds(n, MINOR, stride=both)
+            at_im = pl.ds(n + slots, MINOR, stride=both)
+            turn = twist_ref[n]
+            cos, sin = turn[:, 0:1], turn[:, 1:2]
+            re = jnp.concatenate([sig_lines[at_re, :], ker_lines[at_re, :]], axis=1)
+            im = jnp.concatenate([sig_lines[at_im, :], ker_lines[at_im, :]], axis=1)
+            turned = jnp.concatenate([re * cos + im * sin, im * cos - re * sin], axis=0)
+            spec = dot3(fwd_ref, turned)
+            s_re, k_re = spec[:MINOR, :chans], spec[:MINOR, chans:]
+            s_im, k_im = spec[MINOR:, :chans], spec[MINOR:, chans:]
+            prods.append(
+                jnp.concatenate([s_re * k_re - s_im * k_im, s_re * k_im + s_im * k_re], axis=0)
+            )
+            turns.append((at_re, at_im, cos, sin))
+        back = dot3(inv_ref, jnp.concatenate(prods, axis=1))
+        for d, (at_re, at_im, cos, sin) in enumerate(turns):
+            b_re = back[:MINOR, d * chans : (d + 1) * chans]
+            b_im = back[MINOR:, d * chans : (d + 1) * chans]
+            sig_lines[at_re, :] = b_re * cos - b_im * sin
+            sig_lines[at_im, :] = b_im * cos + b_re * sin
+        return 0
+
+    lax.fori_loop(0, twist_ref.shape[0] // 2, pair, 0)
+
+    def last(i, _):
+        cols = [
+            sig_lines[pl.ds(pl.multiple_of((2 * i + d) * both, 8), both), :] for d in range(2)
+        ]
+        high, low = hi_lo(jnp.concatenate(cols, axis=1))
+        got = jnp.dot(
+            w2_ref[...],
+            jnp.concatenate([high, low, high], axis=0),
+            preferred_element_type=jnp.float32,
+        )
+        for d in range(2):
+            wide_ref[pl.ds(2 * i + d, half, stride=MINOR), :] = got[:, d * chans : (d + 1) * chans]
+        return 0
+
+    lax.fori_loop(0, MINOR // 2, last, 0, unroll=2)
+
+    def narrow(i, _):
+        at = pl.ds(pl.multiple_of(i * piece, piece), piece)
+        out_ref[at, :] = wide_ref[at, :].astype(jnp.bfloat16)
+        return 0
+
+    lax.fori_loop(0, out_ref.shape[0] // piece, narrow, 0)
+
+
+def whole_conv(sig, ker):
+    length, chans = sig.shape
+    half = length // MINOR
+    lines, span = 2 * half, 2 * length
+    classes = half + 1
+    slots = -(-classes // 16) * 16
+    cos, sin = line_tables(lines)
+    w1 = np.zeros((2, slots, half))
+    w1[0, :classes], w1[1, :classes] = cos, -sin
+    w1 = split_table(w1.reshape(2 * slots, half))
+    weight = np.full((classes, 1), 2.0)
+    weight[0] = weight[-1] = 1.0
+    weight /= span
+    w2 = np.zeros((2, slots, half))
+    w2[0, :classes], w2[1, :classes] = weight * cos, -weight * sin
+    w2 = split_table(w2.reshape(2 * slots, half).T)
+    w1 = jnp.concatenate([w1[0], w1[1]], axis=1)
+    w2 = jnp.concatenate([w2[0], w2[0], w2[1]], axis=1)
+    index = np.arange(MINOR)
+    angle = 2 * math.pi / MINOR * (np.outer(index, index) % MINOR)
+    cos, sin = np.cos(angle), np.sin(angle)
+    fwd = split_table(np.block([[cos, sin], [-sin, cos]]))
+    inv = split_table(np.block([[cos, -sin], [sin, cos]]))
+    turn = 2 * math.pi / span * np.outer(np.arange(classes + classes % 2), index)
+    twist = jnp.asarray(np.stack([np.cos(turn), np.sin(turn)], axis=-1), jnp.float32)
+    vmem = pl.BlockSpec(memory_space=pltpu.VMEM)
+    return pl.pallas_call(
+        conv_kernel,
+        in_specs=[vmem] * 7,
+        out_specs=vmem,
+        out_shape=jax.ShapeDtypeStruct((length, chans), jnp.bfloat16),
+        scratch_shapes=[
+            pltpu.VMEM((length, chans), jnp.float32),
+            pltpu.VMEM((MINOR * 2 * slots, chans), jnp.float32),
+            pltpu.VMEM((MINOR * 2 * slots, chans), jnp.float32),
+        ],
+        compiler_params=pltpu.CompilerParams(vmem_limit_bytes=48 * 1024 * 1024),
+        cost_estimate=pl.CostEstimate(
+            flops=classes * 18 * 4 * MINOR * MINOR * chans,
+            bytes_accessed=length * chans * 6,
+            transcendentals=0,
+        ),
+        name="whole_conv",
+    )(w1, w2, fwd, inv, twist, sig, ker)
+
+
+def prepare_kernel(key_ref, value_ref, filter_ref, sig_ref, ker_ref):
+    each = sig_ref.shape[2]
+    for n in range(sig_ref.shape[0]):
+        at = slice(n * each, (n + 1) * each)
+        signal = key_ref[:, at].astype(jnp.float32) * value_ref[:, at].astype(jnp.float32)
+        sig_ref[n] = signal.astype(jnp.bfloat16)
+        ker_ref[n] = filter_ref[:, at]
+
+
+def finish_kernel(gate_ref, key_ref, value_ref, skip_ref, conv_ref, out_ref):
+    each = conv_ref.shape[2]
+    for n in range(conv_ref.shape[0]):
+        at = slice(n * each, (n + 1) * each)
+        signal = key_ref[:, at].astype(jnp.float32) * value_ref[:, at].astype(jnp.float32)
+        out = gate_ref[:, at].astype(jnp.float32) * (
+            conv_ref[n].astype(jnp.float32) + skip_ref[:, at] * signal
+        )
+        out_ref[:, at] = out.astype(jnp.bfloat16)
+
+
+def by_groups(kernel, flat, rowed, pieces, outs, devices, name):
+    rows, chans = flat[0].shape
+    each = chans // devices
+    step = 4 if devices % 4 == 0 else 1
+    whole = pl.BlockSpec((rows, step * each), lambda i: (0, i))
+    thin = pl.BlockSpec((1, step * each), lambda i: (0, i))
+    split = pl.BlockSpec((step, rows, each), lambda i: (i, 0, 0))
+    shape = (devices, rows, each) if outs == 2 else (rows, chans)
+    return pl.pallas_call(
+        kernel,
+        grid=(devices // step,),
+        in_specs=[whole] * len(flat) + [thin] * len(rowed) + [split] * len(pieces),
+        out_specs=[split, split] if outs == 2 else whole,
+        out_shape=[jax.ShapeDtypeStruct(shape, jnp.bfloat16)] * 2
+        if outs == 2
+        else jax.ShapeDtypeStruct(shape, jnp.bfloat16),
+        compiler_params=pltpu.CompilerParams(vmem_limit_bytes=40 * 1024 * 1024),
+        cost_estimate=pl.CostEstimate(
+            flops=rows * chans * 4, bytes_accessed=rows * chans * 10, transcendentals=0
+        ),
+        name=name,
+    )(*flat, *rowed, *pieces)
+
+
+def exchange(x):
+    return lax.all_to_all(x, "seq", split_axis=0, concat_axis=0, tiled=True)
 
 
 def local(
@@ -197,24 +361,54 @@
 ):
     devices = lax.axis_size("seq")
     my_index = lax.axis_index("seq")
+    rows, chans = hyena_key.shape
+    each = chans // devices
+    aligned = each % 128 == 0
     kv_pair = jnp.stack([attn_keys, attn_values])
     behind = lax.ppermute(kv_pair, "seq", [(i, i + 1) for i in range(devices - 1)])
-    ker_blocks = to_channels(long_filter, devices)
-    signal = hyena_key.astype(jnp.float32) * hyena_value.astype(jnp.float32)
-    sig_blocks = to_channels(signal.astype(jnp.bfloat16), devices)
-    window = jnp.concatenate([behind, kv_pair], axis=1)
-    window = lax.all_gather(window, "chan", axis=2, tiled=True)
-    attn_out, attn_lse = attend(attn_query, window[0], window[1], my_index)
-    lines = 2 * ker_blocks.shape[0]
-    ker = spread(ker_blocks)
-    sig = spread(sig_blocks)
-    back = spectra_product(sig, ker, lines * MINOR)
-    conv = to_rows(gather_lines(*back, lines).astype(jnp.bfloat16), devices)
-    signal = hyena_key.astype(jnp.float32) * hyena_value.astype(jnp.float32)
-    hyena_out = hyena_gate.astype(jnp.float32) * (
-        conv.astype(jnp.float32) + skip_weight * signal
-    )
-    return (hyena_out.astype(jnp.bfloat16), attn_out, attn_lse)
+    own = lax.all_gather(kv_pair, "chan", axis=2, tiled=True)
+    if aligned:
+        sig, ker = by_groups(
+            prepare_kernel, (hyena_key, hyena_value, long_filter), (), (), 2, devices, "prepare"
+        )
+    else:
+        signal = hyena_key.astype(jnp.float32) * hyena_value.astype(jnp.float32)
+        sig, ker = (
+            x.reshape(rows, devices, each).transpose(1, 0, 2)
+            for x in (signal.astype(jnp.bfloat16), long_filter)
+        )
+    behind, sig, ker = lax.optimization_barrier((behind, sig, ker))
+    ker, sig = exchange(ker), exchange(sig)
+    behind = lax.all_gather(behind, "chan", axis=2, tiled=True)
+    tokens, groups, features = attn_query.shape
+    queries = attn_query.reshape(tokens * groups, features)
+    out, lse = attend(queries, groups, behind, own, my_index)
+    out, lse, sig, ker = lax.optimization_barrier((out, lse, sig, ker))
+    if aligned:
+        flat = (devices * rows, each)
+        conv = whole_conv(sig.reshape(flat), ker.reshape(flat)).reshape(sig.shape)
+        hyena_out = by_groups(
+            finish_kernel,
+            (hyena_gate, hyena_key, hyena_value),
+            (skip_weight[None, :],),
+            (exchange(conv),),
+            1,
+            devices,
+            "finish",
+        )
+    else:
+        cube = (devices * rows // MINOR, MINOR, each)
+        lines = 2 * cube[0]
+        back = spectra_product(spread(sig.reshape(cube)), spread(ker.reshape(cube)), lines * MINOR)
+        conv = gather_lines(*back, lines).astype(jnp.bfloat16)
+        conv = exchange(conv.reshape(sig.shape)).transpose(1, 0, 2).reshape(rows, chans)
+        signal = hyena_key.astype(jnp.float32) * hyena_value.astype(jnp.float32)
+        hyena_out = hyena_gate.astype(jnp.float32) * (
+            conv.astype(jnp.float32) + skip_weight * signal
+        )
+        hyena_out = hyena_out.astype(jnp.bfloat16)
+    attn_lse = lse.reshape(features // HD, tokens, groups).transpose(2, 0, 1)
+    return (hyena_out, out.reshape(attn_query.shape), attn_lse)
 
 
 def solution(mesh):

time: 335 us -> 294 us (0.88)
  local copies, waits for them, and re-layouts: 78.3 us -> 33.1 us
  Pallas kernels: 77.9 us -> 111 us
  waiting for transfers between devices: 91.2 us -> 112 us
  matrix products: 18.8 us -> 0 us
  starting transfers between devices: 38.3 us -> 21.4 us
  other arithmetic: 14.2 us -> 1.45 us
    all_to_all x3, waiting for transfers between devices: 44.2 us -> 86.9 us  [exchange(): return lax.all_to_all(x, 'seq', split_axis=0, concat_axis=0, tiled=True)]
    pallas_call x1 -> x3, Pallas kernels: 37.3 us -> 74.7 us  [the longest x1 68.8 us: whole_conv(): pl.pallas_call(conv_kernel, in_specs=[vmem] * 7, out_specs=vmem, out_shap...]
    ppermute x1, waiting for transfers between devices: 47 us -> 17.1 us  [local(): lax.ppermute(kv_pair, 'seq', [(i, i + 1) for i in range(devices - 1)])]
    dot_general x4 -> x0, matrix products: 18.8 us -> none  [the longest x2 9.36 us: spread(): jnp.einsum('rpk,kqc->rpqc', wave, blocks.astype(jnp.float32), precision=l...]
    squeeze x3 -> x0, local copies, waits for them, and re-layouts: 16.8 us -> none  [the longest x2 14 us: spread(): return (out[0], out[1])]
    all_to_all x3, starting transfers between devices: 34.7 us -> 18 us  [exchange(): return lax.all_to_all(x, 'seq', split_axis=0, concat_axis=0, tiled=True)]
    convert_element_type x3 -> x0, other arithmetic: 12.6 us -> none  [the longest x1 5.03 us: local(): return (hyena_out.astype(jnp.bfloat16), attn_out, attn_lse)]
    slice x2 -> x0, local copies, waits for them, and re-layouts: 8.93 us -> none  [spread(): return (out[0], out[1])]
  transfers between devices with their start and end apart: 5 -> 6, of which waited for: 2 -> 4; matrix products, arithmetic and copies ran while one was open for 24% -> 5% of each run, Pallas kernels for 23% -> 13%
where the time goes in v2:
time: 294 us; the launch traced here: 293 us
  waiting for transfers between devices  112 us (38%)
  Pallas kernels  111 us (38%)
  local copies, waits for them, and re-layouts  33.1 us (11%)
  starting transfers between devices  21.4 us (7%)
  between operations  14.2 us (5%)
    all_to_all x3, waiting for transfers between devices, exchange(): return lax.all_to_all(x, 'seq', split_axis=0, concat_axis=0, tiled=True)  86.9 us
    pallas_call x1, Pallas kernels, whole_conv(): pl.pallas_call(conv_kernel, in_specs=[vmem] * 7, out_specs=vmem, out_shap...  68.8 us
    pallas_call x1, Pallas kernels, attend(): pl.pallas_call(functools.partial(attend_kernel, groups), grid=(heads,), i...  36.5 us
    unnamed x37, local copies, waits for them, and re-layouts  18.7 us
    all_to_all x3, starting transfers between devices, exchange(): return lax.all_to_all(x, 'seq', split_axis=0, concat_axis=0, tiled=True)  18 us
    ppermute x1, waiting for transfers between devices, local(): lax.ppermute(kv_pair, 'seq', [(i, i + 1) for i in range(devices - 1)])  17.1 us
    reshape x1, local copies, waits for them, and re-layouts, local(): return (hyena_out, out.reshape(attn_query.shape), attn_lse)  7.17 us
    reshape x1, local copies, waits for them, and re-layouts, local(): queries = attn_query.reshape(tokens * groups, features)  6.88 us
  transfers between devices with their start and end apart: 6, of which 4 were waited for; matrix products, arithmetic and copies ran while one was open for 5% of the time, Pallas kernels for 13%

profile of v2, /device:TPU:12, one launch (start us, length us, event | category | flops | bytes accessed | tf_op | source)
XLA Modules:
  0.0 293.2 jit_solution(3156737273500936510)
XLA Ops:
  7.2 1.4 pad_maximum_fusion
  8.6 3.4 %collective-permute-start = (bf16[2,512,512]{2,1,0:T(8,128)(2,1)S(1)}, bf16[2,512,512]{2,1,0:T(8,128)(2,1)}, u32[]{:S(2)}, u32[]{:S(2)}) collective-permute-start(bf16[2,512,512]{2,1,0:T(8,128)(2,1)S(1)} %pad_maximum_fusion), channel_id=1, source_target_pairs={{0,2},{2,4},{4,6},{6,8},{8,10},{10,12},{12,14},{14,16},{16,18},{18... | collective-permute-start | bytes 3145736 | tf_op jit(solution)/shard_map/ppermute | solution.py:368
  12.1 1.6 copy-done.1
  13.6 1.6 copy-done.5
  15.2 1.4 prepare.1
  16.6 1.4 copy-done.6
  18.0 1.3 copy-done.7
  19.3 17.1 %collective-permute-done = bf16[2,512,512]{2,1,0:T(8,128)(2,1)} collective-permute-done((bf16[2,512,512]{2,1,0:T(8,128)(2,1)S(1)}, bf16[2,512,512]{2,1,0:T(8,128)(2,1)}, u32[]{:S(2)}, u32[]{:S(2)}) %collective-permute-start) | collective-permute-done | bytes 1048608 | tf_op jit(solution)/shard_map/ppermute | solution.py:368
  36.4 6.3 %all-to-all-start = ((bf16[16,512,128]{2,1,0:T(8,128)(2,1)}), bf16[16,512,128]{2,1,0:T(8,128)(2,1)}, u32[]{:S(2)}, u32[]{:S(2)}) async-start(bf16[16,512,128]{2,1,0:T(8,128)(2,1)} %copy-done.7), calls=%async_computation | async-start | bytes 4194304 | tf_op jit(solution)/shard_map/all_to_all | solution.py:356
  42.7 0.0 all-gather.5.cloned.1.call-start
  42.7 0.7 all-gather.5.cloned.1.call-update
  43.4 46.9 %all-to-all-done = bf16[16,512,128]{2,1,0:T(8,128)(2,1)} async-done(((bf16[16,512,128]{2,1,0:T(8,128)(2,1)}), bf16[16,512,128]{2,1,0:T(8,128)(2,1)}, u32[]{:S(2)}, u32[]{:S(2)}) %all-to-all-start) | async-done | bytes 2097184 | tf_op jit(solution)/shard_map/all_to_all | solution.py:356
  90.3 4.7 %all-to-all-start.1 = ((bf16[16,512,128]{2,1,0:T(8,128)(2,1)}), bf16[16,512,128]{2,1,0:T(8,128)(2,1)}, u32[]{:S(2)}, u32[]{:S(2)}) async-start(bf16[16,512,128]{2,1,0:T(8,128)(2,1)} %copy-done.6), calls=%async_computation.1 | async-start | bytes 4194304 | tf_op jit(solution)/shard_map/all_to_all | solution.py:356
  95.0 0.0 all-gather.3.cloned.1.call-start
  95.1 0.7 all-gather.3.cloned.1.call-update
  95.8 6.9 %reshape.28.q_ref = bf16[2048,1024]{1,0:T(8,128)(2,1)} reshape(bf16[512,4,1024]{2,1,0:T(4,128)(2,1)} %param.18) | data formatting | bytes 8388608 | tf_op jit(solution)/shard_map/reshape | solution.py:384
  102.7 6.5 %all-gather.3.cloned.1.call-done.kp_ref.vp_ref = bf16[2,512,1024]{2,1,0:T(8,128)(2,1)} async-done(((bf16[2,512,512]{2,1,0:T(8,128)(2,1)}), bf16[2,512,1024]{2,1,0:T(8,128)(2,1)}) %all-gather.3.cloned.1.call-update) | async-done | bytes 2097168 | tf_op jit(solution)/shard_map/all_gather | solution.py:382
  109.2 2.2 copy-done.4
  111.4 1.6 copy-done.11
  112.9 1.6 copy-done.12
  114.5 36.5 %attend.1 = (bf16[2048,1024]{1,0:T(8,128)(2,1)S(1)}, f32[8,1,2048]{2,1,0:T(1,128)S(1)}) custom-call(f32[1,1]{1,0:T(1,128)} %bitcast.1.bias_ref, bf16[2048,1024]{1,0:T(8,128)(2,1)S(1)} %copy-done.4, bf16[2,512,1024]{2,1,0:T(8,128)(2,1)S(1)} %copy-done.12, bf16[2,512,1024]{2,1,0:T(8,128)(2,1)S(1)} %copy-done.12, bf16[2,512,1024]{2,1,0:T(8,128)(2,1)S(1)} %copy-done.11, ...), custom_call_target="tpu_custom_call" | custom-call | flops 8589934592 | bytes 12582912 | tf_op jit(solution)/shard_map/attend/pallas_call | solution.py:155
  151.1 2.0 copy-done.3
  153.1 68.8 %whole_conv.1 = bf16[8192,128]{1,0:T(8,128)(2,1)S(1)} custom-call(bf16[160,128]{1,0:T(8,128)(2,1)S(1)} %copy-done.16, bf16[64,480]{1,0:T(8,128)(2,1)S(1)} %copy-done.15, bf16[2,256,256]{2,1,0:T(8,128)(2,1)S(1)} %copy-done.14, bf16[2,256,256]{2,1,0:T(8,128)(2,1)S(1)} %copy-done.13, f32[66,128,2]{2,1,0:T(8,128)} %constant.26.clone.twist_ref, ...), custom_call_target="tpu_custom_call" | custom-call | flops 9814671360 | bytes 6291456 | tf_op jit(solution)/shard_map/whole_conv/pallas_call | solution.py:291
  221.8 1.3 copy-done.8
  223.2 6.9 %all-to-all-start.2 = ((bf16[16,512,128]{2,1,0:T(8,128)(2,1)}), bf16[16,512,128]{2,1,0:T(8,128)(2,1)}, u32[]{:S(2)}, u32[]{:S(2)}) async-start(bf16[16,512,128]{2,1,0:T(8,128)(2,1)} %bitcast.10), calls=%async_computation.2 | async-start | bytes 4194304 | tf_op jit(solution)/shard_map/all_to_all | solution.py:356
  230.1 0.3 copy.17
  230.5 1.0 copy.18
  231.4 7.2 %reshape.32 = bf16[512,4,1024]{2,1,0:T(4,128)(2,1)} reshape(bf16[2048,1024]{1,0:T(8,128)(2,1)} %copy-done.3) | data formatting | bytes 8388608 | tf_op jit(solution)/shard_map/reshape | solution.py:411
  238.6 40.0 %all-to-all-done.2.conv_ref = bf16[16,512,128]{2,1,0:T(8,128)(2,1)} async-done(((bf16[16,512,128]{2,1,0:T(8,128)(2,1)}), bf16[16,512,128]{2,1,0:T(8,128)(2,1)}, u32[]{:S(2)}, u32[]{:S(2)}) %all-to-all-start.2) | async-done | bytes 2097184 | tf_op jit(solution)/shard_map/all_to_all | solution.py:356
  278.6 1.6 copy-done.2
  280.2 1.6 copy-done.9
  281.8 4.6 %finish.1 = bf16[512,2048]{1,0:T(8,128)(2,1)} custom-call(bf16[512,2048]{1,0:T(8,128)(2,1)S(1)} %copy-done.9, bf16[512,2048]{1,0:T(8,128)(2,1)S(1)} %copy-done, bf16[512,2048]{1,0:T(8,128)(2,1)S(1)} %copy-done.2, f32[1,2048]{1,0:T(1,128)S(1)} %bitcast.11, bf16[16,512,128]{2,1,0:T(8,128)(2,1)} %all-to-all-done.2.conv_ref), custom_call_target="tpu_custom_call" | custom-call | flops 4194304 | bytes 10485760 | tf_op jit(solution)/shard_map/finish/pallas_call | solution.py:339
  (27 shorter events, 0.1 us)
Async XLA Ops:
  7.2 4.9 %copy-start = (bf16[512,2048]{1,0:T(8,128)(2,1)S(1)}, bf16[512,2048]{1,0:T(8,128)(2,1)}, u32[]{:S(2)}) copy-start(bf16[512,2048]{1,0:T(8,128)(2,1)} %key_ref.3) | copy-start | bytes 6291460
  8.6 8.0 %copy-start.17 = (bf16[2,512,512]{2,1,0:T(8,128)(2,1)}, bf16[2,512,512]{2,1,0:T(8,128)(2,1)S(1)}, u32[]{:S(2)}) copy-start(bf16[2,512,512]{2,1,0:T(8,128)(2,1)S(1)} %pad_maximum_fusion) | copy-start | bytes 3145732
  8.6 27.8 %collective-permute-start = (bf16[2,512,512]{2,1,0:T(8,128)(2,1)S(1)}, bf16[2,512,512]{2,1,0:T(8,128)(2,1)}, u32[]{:S(2)}, u32[]{:S(2)}) collective-permute-start(bf16[2,512,512]{2,1,0:T(8,128)(2,1)S(1)} %pad_maximum_fusion), channel_id=1, source_target_pairs={{0,2},{2,4},{4,6},{6,8},{8,10},{10,12},{12,14},{14,16},{16,18},{18... | collective-permute-start | bytes 3145736 | tf_op jit(solution)/shard_map/ppermute | solution.py:368
  12.1 1.6 copy-start.1
  13.6 1.6 copy-start.5
  16.6 1.4 copy-start.6
  18.0 1.3 copy-start.7
  36.4 53.9 %all-to-all-start = ((bf16[16,512,128]{2,1,0:T(8,128)(2,1)}), bf16[16,512,128]{2,1,0:T(8,128)(2,1)}, u32[]{:S(2)}, u32[]{:S(2)}) async-start(bf16[16,512,128]{2,1,0:T(8,128)(2,1)} %copy-done.7), calls=%async_computation | async-start | bytes 4194304 | tf_op jit(solution)/shard_map/all_to_all | solution.py:356
  42.7 60.0 %all-gather.5.cloned.1.call-start = ((), (), s32[]{:S(2)}) async-start(), calls=%async_computation.4 | async-start | bytes 3145728 | tf_op jit(solution)/shard_map/all_gather | solution.py:369
  90.3 62.7 %all-to-all-start.1 = ((bf16[16,512,128]{2,1,0:T(8,128)(2,1)}), bf16[16,512,128]{2,1,0:T(8,128)(2,1)}, u32[]{:S(2)}, u32[]{:S(2)}) async-start(bf16[16,512,128]{2,1,0:T(8,128)(2,1)} %copy-done.6), calls=%async_computation.1 | async-start | bytes 4194304 | tf_op jit(solution)/shard_map/all_to_all | solution.py:356
  95.0 14.1 %all-gather.3.cloned.1.call-start = ((), (), s32[]{:S(2)}) async-start(), calls=%async_computation.3 | async-start | bytes 3145728 | tf_op jit(solution)/shard_map/all_gather | solution.py:382
  109.2 2.2 copy-start.4
  111.4 1.6 copy-start.11
  112.9 1.6 copy-start.12
  114.5 38.5 %copy-start.13 = (bf16[2,256,256]{2,1,0:T(8,128)(2,1)S(1)}, bf16[2,256,256]{2,1,0:T(8,128)(2,1)}, u32[]{:S(2)}) copy-start(bf16[2,256,256]{2,1,0:T(8,128)(2,1)} %constant.25.clone.inv_ref) | copy-start | bytes 786436
  114.5 38.5 %copy-start.14 = (bf16[2,256,256]{2,1,0:T(8,128)(2,1)S(1)}, bf16[2,256,256]{2,1,0:T(8,128)(2,1)}, u32[]{:S(2)}) copy-start(bf16[2,256,256]{2,1,0:T(8,128)(2,1)} %constant.24.clone.fwd_ref) | copy-start | bytes 786436
  114.5 38.5 %copy-start.15 = (bf16[64,480]{1,0:T(8,128)(2,1)S(1)}, bf16[64,480]{1,0:T(8,128)(2,1)}, u32[]{:S(2)}) copy-start(bf16[64,480]{1,0:T(8,128)(2,1)} %constant.36.w2_ref) | copy-start | bytes 184324
  114.5 38.5 %copy-start.16 = (bf16[160,128]{1,0:T(8,128)(2,1)S(1)}, bf16[160,128]{1,0:T(8,128)(2,1)}, u32[]{:S(2)}) copy-start(bf16[160,128]{1,0:T(8,128)(2,1)} %constant.31.w1_ref) | copy-start | bytes 122884
  151.1 2.0 copy-start.3
  221.8 1.3 copy-start.8
  223.2 55.5 %all-to-all-start.2 = ((bf16[16,512,128]{2,1,0:T(8,128)(2,1)}), bf16[16,512,128]{2,1,0:T(8,128)(2,1)}, u32[]{:S(2)}, u32[]{:S(2)}) async-start(bf16[16,512,128]{2,1,0:T(8,128)(2,1)} %bitcast.10), calls=%async_computation.2 | async-start | bytes 4194304 | tf_op jit(solution)/shard_map/all_to_all | solution.py:356
  231.4 47.2 %copy-start.10 = (f32[2048]{0:T(1024)S(1)}, f32[2048]{0:T(1024)}, u32[]{:S(2)}) copy-start(f32[2048]{0:T(1024)} %param.17) | copy-start | bytes 24580
  278.6 1.6 copy-start.2
  280.2 1.6 copy-start.9
Sparse Core Ops, SparseCore 0:
  45.1 11.6 all-gather.4
  97.4 11.6 all-gather.2

commit v3 on v2

--- a/solution.py
+++ b/solution.py
@@ -178,22 +178,22 @@
     )(bias, queries, behind, behind, own, own)
 
 
-def conv_kernel(w1_ref, w2_ref, fwd_ref, inv_ref, twist_ref, sig_ref, ker_ref, out_ref,
+def conv_kernel(w1_ref, w2_ref, fwd_ref, inv_ref, twist_ref, both_ref, out_ref,
                 wide_ref, sig_lines, ker_lines):
-    half = sig_ref.shape[0] // MINOR
+    devices, rows = both_ref.shape[0], both_ref.shape[1] // 2
+    half = wide_ref.shape[0] // MINOR
     both = w1_ref.shape[0]
     slots = both // 2
-    chans = sig_ref.shape[1]
-    piece = min(1024, sig_ref.shape[0])
-
-    for source, lines in ((sig_ref, sig_lines), (ker_ref, ker_lines)):
+    chans = wide_ref.shape[1]
+
+    for offset, lines in ((0, sig_lines), (rows, ker_lines)):
 
         def widen(i, _):
-            at = pl.ds(pl.multiple_of(i * piece, piece), piece)
-            wide_ref[at, :] = source[at, :].astype(jnp.float32)
+            at = pl.ds(pl.multiple_of(i * rows, rows), rows)
+            wide_ref[at, :] = both_ref[i, offset : offset + rows, :].astype(jnp.float32)
             return 0
 
-        lax.fori_loop(0, source.shape[0] // piece, widen, 0)
+        lax.fori_loop(0, devices, widen, 0)
 
         def first(i, _):
             cols = [wide_ref[pl.ds(2 * i + d, half, stride=MINOR), :] for d in range(2)]
@@ -208,18 +208,20 @@
                 lines[at, :] = got[:, d * chans : (d + 1) * chans]
             return 0
 
-        lax.fori_loop(0, MINOR // 2, first, 0, unroll=2)
-
-    def pair(i, _):
-        prods, turns = [], []
-        for d in range(2):
-            n = 2 * i + d
+        lax.fori_loop(0, MINOR // 2, first, 0, unroll=4)
+
+    def several(i, _):
+        loaded = []
+        for d in range(4):
+            n = 4 * i + d
             at_re = pl.ds(n, MINOR, stride=both)
             at_im = pl.ds(n + slots, MINOR, stride=both)
             turn = twist_ref[n]
-            cos, sin = turn[:, 0:1], turn[:, 1:2]
             re = jnp.concatenate([sig_lines[at_re, :], ker_lines[at_re, :]], axis=1)
             im = jnp.concatenate([sig_lines[at_im, :], ker_lines[at_im, :]], axis=1)
+            loaded.append((at_re, at_im, turn[:, 0:1], turn[:, 1:2], re, im))
+        prods = []
+        for _, _, cos, sin, re, im in loaded:
             turned = jnp.concatenate([re * cos + im * sin, im * cos - re * sin], axis=0)
             spec = dot3(fwd_ref, turned)
             s_re, k_re = spec[:MINOR, :chans], spec[:MINOR, chans:]
@@ -227,16 +229,15 @@
             prods.append(
                 jnp.concatenate([s_re * k_re - s_im * k_im, s_re * k_im + s_im * k_re], axis=0)
             )
-            turns.append((at_re, at_im, cos, sin))
-        back = dot3(inv_ref, jnp.concatenate(prods, axis=1))
-        for d, (at_re, at_im, cos, sin) in enumerate(turns):
-            b_re = back[:MINOR, d * chans : (d + 1) * chans]
-            b_im = back[MINOR:, d * chans : (d + 1) * chans]
+        backs = [dot3(inv_ref, jnp.concatenate(prods[d : d + 2], axis=1)) for d in (0, 2)]
+        for d, (at_re, at_im, cos, sin, _, _) in enumerate(loaded):
+            back = backs[d // 2][:, (d % 2) * chans : (d % 2 + 1) * chans]
+            b_re, b_im = back[:MINOR], back[MINOR:]
             sig_lines[at_re, :] = b_re * cos - b_im * sin
             sig_lines[at_im, :] = b_im * cos + b_re * sin
         return 0
 
-    lax.fori_loop(0, twist_ref.shape[0] // 2, pair, 0)
+    lax.fori_loop(0, twist_ref.shape[0] // 4, several, 0)
 
     def last(i, _):
         cols = [
@@ -252,22 +253,24 @@
             wide_ref[pl.ds(2 * i + d, half, stride=MINOR), :] = got[:, d * chans : (d + 1) * chans]
         return 0
 
-    lax.fori_loop(0, MINOR // 2, last, 0, unroll=2)
+    lax.fori_loop(0, MINOR // 2, last, 0, unroll=4)
 
     def narrow(i, _):
-        at = pl.ds(pl.multiple_of(i * piece, piece), piece)
-        out_ref[at, :] = wide_ref[at, :].astype(jnp.bfloat16)
+        at = pl.ds(pl.multiple_of(i * rows, rows), rows)
+        out_ref[i] = wide_ref[at, :].astype(jnp.bfloat16)
         return 0
 
-    lax.fori_loop(0, out_ref.shape[0] // piece, narrow, 0)
-
-
-def whole_conv(sig, ker):
-    length, chans = sig.shape
+    lax.fori_loop(0, devices, narrow, 0)
+
+
+def whole_conv(both):
+    devices, rows, chans = both.shape
+    rows = rows // 2
+    length = devices * rows
     half = length // MINOR
     lines, span = 2 * half, 2 * length
     classes = half + 1
-    slots = -(-classes // 16) * 16
+    slots = -(-classes // 8) * 8
     cos, sin = line_tables(lines)
     w1 = np.zeros((2, slots, half))
     w1[0, :classes], w1[1, :classes] = cos, -sin
@@ -285,14 +288,14 @@
     cos, sin = np.cos(angle), np.sin(angle)
     fwd = split_table(np.block([[cos, sin], [-sin, cos]]))
     inv = split_table(np.block([[cos, -sin], [sin, cos]]))
-    turn = 2 * math.pi / span * np.outer(np.arange(classes + classes % 2), index)
+    turn = 2 * math.pi / span * np.outer(np.arange(-(-classes // 4) * 4), index)
     twist = jnp.asarray(np.stack([np.cos(turn), np.sin(turn)], axis=-1), jnp.float32)
     vmem = pl.BlockSpec(memory_space=pltpu.VMEM)
     return pl.pallas_call(
         conv_kernel,
-        in_specs=[vmem] * 7,
+        in_specs=[vmem] * 6,
         out_specs=vmem,
-        out_shape=jax.ShapeDtypeStruct((length, chans), jnp.bfloat16),
+        out_shape=jax.ShapeDtypeStruct((devices, rows, chans), jnp.bfloat16),
         scratch_shapes=[
             pltpu.VMEM((length, chans), jnp.float32),
             pltpu.VMEM((MINOR * 2 * slots, chans), jnp.float32),
@@ -305,16 +308,16 @@
             transcendentals=0,
         ),
         name="whole_conv",
-    )(w1, w2, fwd, inv, twist, sig, ker)
-
-
-def prepare_kernel(key_ref, value_ref, filter_ref, sig_ref, ker_ref):
-    each = sig_ref.shape[2]
-    for n in range(sig_ref.shape[0]):
+    )(w1, w2, fwd, inv, twist, both)
+
+
+def prepare_kernel(key_ref, value_ref, filter_ref, both_ref):
+    rows, each = key_ref.shape[0], both_ref.shape[2]
+    for n in range(both_ref.shape[0]):
         at = slice(n * each, (n + 1) * each)
         signal = key_ref[:, at].astype(jnp.float32) * value_ref[:, at].astype(jnp.float32)
-        sig_ref[n] = signal.astype(jnp.bfloat16)
-        ker_ref[n] = filter_ref[:, at]
+        both_ref[n, :rows] = signal.astype(jnp.bfloat16)
+        both_ref[n, rows:] = filter_ref[:, at]
 
 
 def finish_kernel(gate_ref, key_ref, value_ref, skip_ref, conv_ref, out_ref):
@@ -328,22 +331,20 @@
         out_ref[:, at] = out.astype(jnp.bfloat16)
 
 
-def by_groups(kernel, flat, rowed, pieces, outs, devices, name):
+def by_groups(kernel, flat, rowed, pieces, shape, devices, name):
     rows, chans = flat[0].shape
     each = chans // devices
     step = 4 if devices % 4 == 0 else 1
     whole = pl.BlockSpec((rows, step * each), lambda i: (0, i))
     thin = pl.BlockSpec((1, step * each), lambda i: (0, i))
     split = pl.BlockSpec((step, rows, each), lambda i: (i, 0, 0))
-    shape = (devices, rows, each) if outs == 2 else (rows, chans)
+    widened = pl.BlockSpec((step, 2 * rows, each), lambda i: (i, 0, 0))
     return pl.pallas_call(
         kernel,
         grid=(devices // step,),
         in_specs=[whole] * len(flat) + [thin] * len(rowed) + [split] * len(pieces),
-        out_specs=[split, split] if outs == 2 else whole,
-        out_shape=[jax.ShapeDtypeStruct(shape, jnp.bfloat16)] * 2
-        if outs == 2
-        else jax.ShapeDtypeStruct(shape, jnp.bfloat16),
+        out_specs=whole if len(shape) == 2 else widened,
+        out_shape=jax.ShapeDtypeStruct(shape, jnp.bfloat16),
         compiler_params=pltpu.CompilerParams(vmem_limit_bytes=40 * 1024 * 1024),
         cost_estimate=pl.CostEstimate(
             flops=rows * chans * 4, bytes_accessed=rows * chans * 10, transcendentals=0
@@ -368,40 +369,44 @@
     behind = lax.ppermute(kv_pair, "seq", [(i, i + 1) for i in range(devices - 1)])
     own = lax.all_gather(kv_pair, "chan", axis=2, tiled=True)
     if aligned:
-        sig, ker = by_groups(
-            prepare_kernel, (hyena_key, hyena_value, long_filter), (), (), 2, devices, "prepare"
+        both = by_groups(
+            prepare_kernel,
+            (hyena_key, hyena_value, long_filter),
+            (),
+            (),
+            (devices, 2 * rows, each),
+            devices,
+            "prepare",
         )
     else:
         signal = hyena_key.astype(jnp.float32) * hyena_value.astype(jnp.float32)
-        sig, ker = (
-            x.reshape(rows, devices, each).transpose(1, 0, 2)
-            for x in (signal.astype(jnp.bfloat16), long_filter)
-        )
-    behind, sig, ker = lax.optimization_barrier((behind, sig, ker))
-    ker, sig = exchange(ker), exchange(sig)
+        both = jnp.concatenate([signal.astype(jnp.bfloat16), long_filter], axis=0)
+        both = both.reshape(2 * rows, devices, each).transpose(1, 0, 2)
+    behind, both = lax.optimization_barrier((behind, both))
+    both = exchange(both)
     behind = lax.all_gather(behind, "chan", axis=2, tiled=True)
     tokens, groups, features = attn_query.shape
     queries = attn_query.reshape(tokens * groups, features)
     out, lse = attend(queries, groups, behind, own, my_index)
-    out, lse, sig, ker = lax.optimization_barrier((out, lse, sig, ker))
+    out, lse, both = lax.optimization_barrier((out, lse, both))
     if aligned:
-        flat = (devices * rows, each)
-        conv = whole_conv(sig.reshape(flat), ker.reshape(flat)).reshape(sig.shape)
+        conv = whole_conv(both)
         hyena_out = by_groups(
             finish_kernel,
             (hyena_gate, hyena_key, hyena_value),
             (skip_weight[None, :],),
             (exchange(conv),),
-            1,
+            (rows, chans),
             devices,
             "finish",
         )
     else:
         cube = (devices * rows // MINOR, MINOR, each)
         lines = 2 * cube[0]
-        back = spectra_product(spread(sig.reshape(cube)), spread(ker.reshape(cube)), lines * MINOR)
+        sig, ker = both[:, :rows].reshape(cube), both[:, rows:].reshape(cube)
+        back = spectra_product(spread(sig), spread(ker), lines * MINOR)
         conv = gather_lines(*back, lines).astype(jnp.bfloat16)
-        conv = exchange(conv.reshape(sig.shape)).transpose(1, 0, 2).reshape(rows, chans)
+        conv = exchange(conv.reshape(devices, rows, each)).transpose(1, 0, 2).reshape(rows, chans)
         signal = hyena_key.astype(jnp.float32) * hyena_value.astype(jnp.float32)
         hyena_out = hyena_gate.astype(jnp.float32) * (
             conv.astype(jnp.float32) + skip_weight * signal

time: 294 us -> 249 us (0.85)
  Pallas kernels: 111 us -> 86.4 us
  waiting for transfers between devices: 112 us -> 97.9 us
  starting transfers between devices: 21.4 us -> 15.4 us
    all_to_all x3 -> x2, waiting for transfers between devices: 86.9 us -> 59.2 us  [exchange(): return lax.all_to_all(x, 'seq', split_axis=0, concat_axis=0, tiled=True)]
    pallas_call x1, Pallas kernels: 68.8 us -> 43.9 us  [whole_conv(): pl.pallas_call(conv_kernel, in_specs=[vmem] * 6, out_specs=vmem, out_shap...]
    all_gather x1, waiting for transfers between devices: 6.49 us -> 13.3 us  [local(): behind = lax.all_gather(behind, 'chan', axis=2, tiled=True)]
    all_gather x1, waiting for transfers between devices: 0.01 us -> 6.23 us  [local(): own = lax.all_gather(kv_pair, 'chan', axis=2, tiled=True)]
    all_to_all x3 -> x2, starting transfers between devices: 18 us -> 11.9 us  [exchange(): return lax.all_to_all(x, 'seq', split_axis=0, concat_axis=0, tiled=True)]
    unnamed x37 -> x35, local copies, waits for them, and re-layouts: 18.7 us -> 18.1 us
  transfers between devices with their start and end apart: 6 -> 5, of which waited for: 4 -> 5; matrix products, arithmetic and copies ran while one was open for 5% -> 6% of each run, Pallas kernels for 13% -> 15%
where the time goes in v3:
time: 249 us; the launch traced here: 248 us
  waiting for transfers between devices  97.9 us (39%)
  Pallas kernels  86.4 us (35%)
  local copies, waits for them, and re-layouts  32.6 us (13%)
  starting transfers between devices  15.4 us (6%)
  between operations  14.2 us (6%)
    all_to_all x2, waiting for transfers between devices, exchange(): return lax.all_to_all(x, 'seq', split_axis=0, concat_axis=0, tiled=True)  59.2 us
    pallas_call x1, Pallas kernels, whole_conv(): pl.pallas_call(conv_kernel, in_specs=[vmem] * 6, out_specs=vmem, out_shap...  43.9 us
    pallas_call x1, Pallas kernels, attend(): pl.pallas_call(functools.partial(attend_kernel, groups), grid=(heads,), i...  36.5 us
    unnamed x35, local copies, waits for them, and re-layouts  18.1 us
    ppermute x1, waiting for transfers between devices, local(): lax.ppermute(kv_pair, 'seq', [(i, i + 1) for i in range(devices - 1)])  17.8 us
    all_gather x1, waiting for transfers between devices, local(): behind = lax.all_gather(behind, 'chan', axis=2, tiled=True)  13.3 us
    all_to_all x2, starting transfers between devices, exchange(): return lax.all_to_all(x, 'seq', split_axis=0, concat_axis=0, tiled=True)  11.9 us
    reshape x1, local copies, waits for them, and re-layouts, local(): return (hyena_out, out.reshape(attn_query.shape), attn_lse)  7.17 us
  transfers between devices with their start and end apart: 5, of which 5 were waited for; matrix products, arithmetic and copies ran while one was open for 6% of the time, Pallas kernels for 15%

profile of v3, /device:TPU:12, one launch (start us, length us, event | category | flops | bytes accessed | tf_op | source)
XLA Modules:
  0.0 247.9 jit_solution(2842891099343961270)
XLA Ops:
  7.2 1.4 pad_maximum_fusion
  8.6 3.4 %collective-permute-start = (bf16[2,512,512]{2,1,0:T(8,128)(2,1)S(1)}, bf16[2,512,512]{2,1,0:T(8,128)(2,1)}, u32[]{:S(2)}, u32[]{:S(2)}) collective-permute-start(bf16[2,512,512]{2,1,0:T(8,128)(2,1)S(1)} %pad_maximum_fusion), channel_id=1, source_target_pairs={{0,2},{2,4},{4,6},{6,8},{8,10},{10,12},{12,14},{14,16},{16,18},{18... | collective-permute-start | bytes 3145736 | tf_op jit(solution)/shard_map/ppermute | solution.py:369
  12.1 1.6 copy-done.2
  13.7 1.6 copy-done.6
  15.2 1.4 prepare.1
  16.6 2.0 copy-done
  18.7 17.8 %collective-permute-done = bf16[2,512,512]{2,1,0:T(8,128)(2,1)} collective-permute-done((bf16[2,512,512]{2,1,0:T(8,128)(2,1)S(1)}, bf16[2,512,512]{2,1,0:T(8,128)(2,1)}, u32[]{:S(2)}, u32[]{:S(2)}) %collective-permute-start) | collective-permute-done | bytes 1048608 | tf_op jit(solution)/shard_map/ppermute | solution.py:369
  36.4 6.3 %all-to-all-start = ((bf16[16,1024,128]{2,1,0:T(8,128)(2,1)}), bf16[16,1024,128]{2,1,0:T(8,128)(2,1)}, u32[]{:S(2)}, u32[]{:S(2)}) async-start(bf16[16,1024,128]{2,1,0:T(8,128)(2,1)} %copy-done), calls=%async_computation | async-start | bytes 8388608 | tf_op jit(solution)/shard_map/all_to_all | solution.py:357
  42.7 0.0 all-gather.5.cloned.1.call-start
  42.7 0.7 all-gather.5.cloned.1.call-update
  43.4 0.0 all-gather.3.cloned.1.call-start
  43.5 0.7 all-gather.3.cloned.1.call-update
  44.2 7.0 %reshape.19.q_ref = bf16[2048,1024]{1,0:T(8,128)(2,1)} reshape(bf16[512,4,1024]{2,1,0:T(4,128)(2,1)} %param.18) | data formatting | bytes 8388608 | tf_op jit(solution)/shard_map/reshape | solution.py:389
  51.2 6.2 %all-gather.5.cloned.1.call-done.ko_ref.vo_ref = bf16[2,512,1024]{2,1,0:T(8,128)(2,1)} async-done(((bf16[2,512,512]{2,1,0:T(8,128)(2,1)}), bf16[2,512,1024]{2,1,0:T(8,128)(2,1)}) %all-gather.5.cloned.1.call-update) | async-done | bytes 2097168 | tf_op jit(solution)/shard_map/all_gather | solution.py:370
  57.4 13.3 %all-gather.3.cloned.1.call-done.kp_ref.vp_ref = bf16[2,512,1024]{2,1,0:T(8,128)(2,1)} async-done(((bf16[2,512,512]{2,1,0:T(8,128)(2,1)}), bf16[2,512,1024]{2,1,0:T(8,128)(2,1)}) %all-gather.3.cloned.1.call-update) | async-done | bytes 2097168 | tf_op jit(solution)/shard_map/all_gather | solution.py:387
  70.7 2.2 copy-done.5
  72.9 1.6 copy-done.10
  74.5 1.6 copy-done.11
  76.1 36.5 %attend.1 = (bf16[2048,1024]{1,0:T(8,128)(2,1)S(1)}, f32[8,1,2048]{2,1,0:T(1,128)S(1)}) custom-call(f32[1,1]{1,0:T(1,128)} %bitcast.1.bias_ref, bf16[2048,1024]{1,0:T(8,128)(2,1)S(1)} %copy-done.5, bf16[2,512,1024]{2,1,0:T(8,128)(2,1)S(1)} %copy-done.11, bf16[2,512,1024]{2,1,0:T(8,128)(2,1)S(1)} %copy-done.11, bf16[2,512,1024]{2,1,0:T(8,128)(2,1)S(1)} %copy-done.10, ...), custom_call_target="tpu_custom_call" | custom-call | flops 8589934592 | bytes 12582912 | tf_op jit(solution)/shard_map/attend/pallas_call | solution.py:155
  112.6 2.0 copy-done.4
  114.6 20.0 %all-to-all-done.both_ref = bf16[16,1024,128]{2,1,0:T(8,128)(2,1)} async-done(((bf16[16,1024,128]{2,1,0:T(8,128)(2,1)}), bf16[16,1024,128]{2,1,0:T(8,128)(2,1)}, u32[]{:S(2)}, u32[]{:S(2)}) %all-to-all-start) | async-done | bytes 4194336 | tf_op jit(solution)/shard_map/all_to_all | solution.py:357
  134.7 43.9 %whole_conv.1 = bf16[16,512,128]{2,1,0:T(8,128)(2,1)S(1)} custom-call(bf16[144,128]{1,0:T(8,128)(2,1)S(1)} %copy-done.15, bf16[64,432]{1,0:T(8,128)(2,1)S(1)} %copy-done.14, bf16[2,256,256]{2,1,0:T(8,128)(2,1)S(1)} %copy-done.13, bf16[2,256,256]{2,1,0:T(8,128)(2,1)S(1)} %copy-done.12, f32[68,128,2]{2,1,0:T(8,128)} %constant.26.clone.twist_ref, ...), custom_call_target="tpu_custom_call" | custom-call | flops 9814671360 | bytes 6291456 | tf_op jit(solution)/shard_map/whole_conv/pallas_call | solution.py:294
  178.6 0.0 copy-start.7
  178.6 1.3 copy-done.7
  179.9 5.7 %all-to-all-start.1 = ((bf16[16,512,128]{2,1,0:T(8,128)(2,1)}), bf16[16,512,128]{2,1,0:T(8,128)(2,1)}, u32[]{:S(2)}, u32[]{:S(2)}) async-start(bf16[16,512,128]{2,1,0:T(8,128)(2,1)} %copy-done.7), calls=%async_computation.1 | async-start | bytes 4194304 | tf_op jit(solution)/shard_map/all_to_all | solution.py:357
  185.6 0.3 copy.17
  186.0 1.0 copy.18
  186.9 7.2 %reshape.20 = bf16[512,4,1024]{2,1,0:T(4,128)(2,1)} reshape(bf16[2048,1024]{1,0:T(8,128)(2,1)} %copy-done.4) | data formatting | bytes 8388608 | tf_op jit(solution)/shard_map/reshape | solution.py:416
  194.1 39.2 %all-to-all-done.1.conv_ref = bf16[16,512,128]{2,1,0:T(8,128)(2,1)} async-done(((bf16[16,512,128]{2,1,0:T(8,128)(2,1)}), bf16[16,512,128]{2,1,0:T(8,128)(2,1)}, u32[]{:S(2)}, u32[]{:S(2)}) %all-to-all-start.1) | async-done | bytes 2097184 | tf_op jit(solution)/shard_map/all_to_all | solution.py:357
  233.3 1.6 copy-done.3
  234.9 1.6 copy-done.8
  236.5 4.6 %finish.1 = bf16[512,2048]{1,0:T(8,128)(2,1)} custom-call(bf16[512,2048]{1,0:T(8,128)(2,1)S(1)} %copy-done.8, bf16[512,2048]{1,0:T(8,128)(2,1)S(1)} %copy-done.1, bf16[512,2048]{1,0:T(8,128)(2,1)S(1)} %copy-done.3, f32[1,2048]{1,0:T(1,128)S(1)} %bitcast.7, bf16[16,512,128]{2,1,0:T(8,128)(2,1)} %all-to-all-done.1.conv_ref), custom_call_target="tpu_custom_call" | custom-call | flops 4194304 | bytes 10485760 | tf_op jit(solution)/shard_map/finish/pallas_call | solution.py:342
  (23 shorter events, 0.0 us)
Async XLA Ops:
  7.2 4.9 %copy-start.1 = (bf16[512,2048]{1,0:T(8,128)(2,1)S(1)}, bf16[512,2048]{1,0:T(8,128)(2,1)}, u32[]{:S(2)}) copy-start(bf16[512,2048]{1,0:T(8,128)(2,1)} %key_ref.3) | copy-start | bytes 6291460
  8.6 8.0 %copy-start.16 = (bf16[2,512,512]{2,1,0:T(8,128)(2,1)}, bf16[2,512,512]{2,1,0:T(8,128)(2,1)S(1)}, u32[]{:S(2)}) copy-start(bf16[2,512,512]{2,1,0:T(8,128)(2,1)S(1)} %pad_maximum_fusion) | copy-start | bytes 3145732
  8.6 27.8 %collective-permute-start = (bf16[2,512,512]{2,1,0:T(8,128)(2,1)S(1)}, bf16[2,512,512]{2,1,0:T(8,128)(2,1)}, u32[]{:S(2)}, u32[]{:S(2)}) collective-permute-start(bf16[2,512,512]{2,1,0:T(8,128)(2,1)S(1)} %pad_maximum_fusion), channel_id=1, source_target_pairs={{0,2},{2,4},{4,6},{6,8},{8,10},{10,12},{12,14},{14,16},{16,18},{18... | collective-permute-start | bytes 3145736 | tf_op jit(solution)/shard_map/ppermute | solution.py:369
  12.1 1.6 copy-start.2
  13.6 1.6 copy-start.6
  16.6 2.0 copy-start
  36.4 98.2 %all-to-all-start = ((bf16[16,1024,128]{2,1,0:T(8,128)(2,1)}), bf16[16,1024,128]{2,1,0:T(8,128)(2,1)}, u32[]{:S(2)}, u32[]{:S(2)}) async-start(bf16[16,1024,128]{2,1,0:T(8,128)(2,1)} %copy-done), calls=%async_computation | async-start | bytes 8388608 | tf_op jit(solution)/shard_map/all_to_all | solution.py:357
  42.7 14.7 %all-gather.5.cloned.1.call-start = ((), (), s32[]{:S(2)}) async-start(), calls=%async_computation.3 | async-start | bytes 3145728 | tf_op jit(solution)/shard_map/all_gather | solution.py:370
  43.4 27.3 %all-gather.3.cloned.1.call-start = ((), (), s32[]{:S(2)}) async-start(), calls=%async_computation.2 | async-start | bytes 3145728 | tf_op jit(solution)/shard_map/all_gather | solution.py:387
  70.7 2.2 copy-start.5
  72.9 1.6 copy-start.10
  74.5 1.6 copy-start.11
  76.1 58.6 %copy-start.12 = (bf16[2,256,256]{2,1,0:T(8,128)(2,1)S(1)}, bf16[2,256,256]{2,1,0:T(8,128)(2,1)}, u32[]{:S(2)}) copy-start(bf16[2,256,256]{2,1,0:T(8,128)(2,1)} %constant.25.clone.inv_ref) | copy-start | bytes 786436
  76.1 58.6 %copy-start.13 = (bf16[2,256,256]{2,1,0:T(8,128)(2,1)S(1)}, bf16[2,256,256]{2,1,0:T(8,128)(2,1)}, u32[]{:S(2)}) copy-start(bf16[2,256,256]{2,1,0:T(8,128)(2,1)} %constant.24.clone.fwd_ref) | copy-start | bytes 786436
  76.1 58.6 %copy-start.14 = (bf16[64,432]{1,0:T(8,128)(2,1)S(1)}, bf16[64,432]{1,0:T(8,128)(2,1)}, u32[]{:S(2)}) copy-start(bf16[64,432]{1,0:T(8,128)(2,1)} %constant.36.w2_ref) | copy-start | bytes 165892
  76.1 58.6 %copy-start.15 = (bf16[144,128]{1,0:T(8,128)(2,1)S(1)}, bf16[144,128]{1,0:T(8,128)(2,1)}, u32[]{:S(2)}) copy-start(bf16[144,128]{1,0:T(8,128)(2,1)} %constant.31.w1_ref) | copy-start | bytes 110596
  112.6 2.0 copy-start.4
  178.6 1.3 copy-start.7
  179.9 53.4 %all-to-all-start.1 = ((bf16[16,512,128]{2,1,0:T(8,128)(2,1)}), bf16[16,512,128]{2,1,0:T(8,128)(2,1)}, u32[]{:S(2)}, u32[]{:S(2)}) async-start(bf16[16,512,128]{2,1,0:T(8,128)(2,1)} %copy-done.7), calls=%async_computation.1 | async-start | bytes 4194304 | tf_op jit(solution)/shard_map/all_to_all | solution.py:357
  186.9 46.4 %copy-start.9 = (f32[2048]{0:T(1024)S(1)}, f32[2048]{0:T(1024)}, u32[]{:S(2)}) copy-start(f32[2048]{0:T(1024)} %param.17) | copy-start | bytes 24580
  233.3 1.6 copy-start.3
  234.9 1.6 copy-start.8
Sparse Core Ops, SparseCore 0:
  45.7 11.6 all-gather.4
  58.9 11.7 all-gather.2

commit v4 on v3

--- a/solution.py
+++ b/solution.py
@@ -178,85 +178,96 @@
     )(bias, queries, behind, behind, own, own)
 
 
-def conv_kernel(w1_ref, w2_ref, fwd_ref, inv_ref, twist_ref, both_ref, out_ref,
-                wide_ref, sig_lines, ker_lines):
-    devices, rows = both_ref.shape[0], both_ref.shape[1] // 2
+def conv_kernel(w1_ref, w2_ref, fwd_ref, inv_ref, twist_ref, both_ref, out_ref, wide_ref, lines):
+    devices, rows, chans = both_ref.shape
     half = wide_ref.shape[0] // MINOR
     both = w1_ref.shape[0]
     slots = both // 2
-    chans = wide_ref.shape[1]
-
-    for offset, lines in ((0, sig_lines), (rows, ker_lines)):
-
-        def widen(i, _):
-            at = pl.ds(pl.multiple_of(i * rows, rows), rows)
-            wide_ref[at, :] = both_ref[i, offset : offset + rows, :].astype(jnp.float32)
-            return 0
-
-        lax.fori_loop(0, devices, widen, 0)
-
-        def first(i, _):
-            cols = [wide_ref[pl.ds(2 * i + d, half, stride=MINOR), :] for d in range(2)]
-            col = jnp.concatenate(cols, axis=1).astype(jnp.bfloat16)
-            got = jnp.dot(
-                w1_ref[...],
-                jnp.concatenate([col, col], axis=0),
-                preferred_element_type=jnp.float32,
-            )
-            for d in range(2):
-                at = pl.ds(pl.multiple_of((2 * i + d) * both, 8), both)
-                lines[at, :] = got[:, d * chans : (d + 1) * chans]
-            return 0
-
-        lax.fori_loop(0, MINOR // 2, first, 0, unroll=4)
+    kept = w2_ref.shape[1] // 6
+    middle = chans // 2
+    left = lax.broadcasted_iota(jnp.int32, (1, chans), 1) < middle
+    swap = lambda x: pltpu.roll(x, middle, 1)
+
+    def widen(i, _):
+        at = pl.ds(pl.multiple_of(i * rows, rows), rows)
+        wide_ref[at, :] = both_ref[i].astype(jnp.float32)
+        return 0
+
+    lax.fori_loop(0, devices, widen, 0)
+
+    def first(i, _):
+        cols = [wide_ref[pl.ds(2 * i + d, half, stride=MINOR), :] for d in range(2)]
+        col = jnp.concatenate(cols, axis=1).astype(jnp.bfloat16)
+        got = jnp.dot(
+            w1_ref[...], jnp.concatenate([col, col], axis=0), preferred_element_type=jnp.float32
+        )
+        for d in range(2):
+            at = pl.ds(pl.multiple_of((2 * i + d) * both, 8), both)
+            lines[at, :] = got[:, d * chans : (d + 1) * chans]
+        return 0
+
+    lax.fori_loop(0, MINOR // 2, first, 0, unroll=4)
 
     def several(i, _):
-        loaded = []
+        turned, turns = [], []
         for d in range(4):
             n = 4 * i + d
-            at_re = pl.ds(n, MINOR, stride=both)
-            at_im = pl.ds(n + slots, MINOR, stride=both)
+            re = lines[pl.ds(n, MINOR, stride=both), :]
+            im = lines[pl.ds(n + slots, MINOR, stride=both), :]
             turn = twist_ref[n]
-            re = jnp.concatenate([sig_lines[at_re, :], ker_lines[at_re, :]], axis=1)
-            im = jnp.concatenate([sig_lines[at_im, :], ker_lines[at_im, :]], axis=1)
-            loaded.append((at_re, at_im, turn[:, 0:1], turn[:, 1:2], re, im))
+            cos, sin = turn[:, 0:1], turn[:, 1:2]
+            turned.append(jnp.concatenate([re * cos + im * sin, im * cos - re * sin], axis=0))
+            turns.append((cos, sin))
         prods = []
-        for _, _, cos, sin, re, im in loaded:
-            turned = jnp.concatenate([re * cos + im * sin, im * cos - re * sin], axis=0)
-            spec = dot3(fwd_ref, turned)
-            s_re, k_re = spec[:MINOR, :chans], spec[:MINOR, chans:]
-            s_im, k_im = spec[MINOR:, :chans], spec[MINOR:, chans:]
-            prods.append(
-                jnp.concatenate([s_re * k_re - s_im * k_im, s_re * k_im + s_im * k_re], axis=0)
+        for d in (0, 2):
+            spec = dot3(fwd_ref, jnp.concatenate(turned[d : d + 2], axis=1))
+            pair = []
+            for x in (spec[:, :chans], spec[:, chans:]):
+                y = swap(x)
+                re, im, re2, im2 = x[:MINOR], x[MINOR:], y[:MINOR], y[MINOR:]
+                pair.append(jnp.concatenate([re * re2 - im * im2, re * im2 + im * re2], axis=0))
+            prods.append(jnp.where(left, pair[0], pair[1]))
+        back = dot3(inv_ref, jnp.concatenate(prods, axis=1))
+        for d in range(2):
+            b_re = back[:MINOR, d * chans : (d + 1) * chans]
+            b_im = back[MINOR:, d * chans : (d + 1) * chans]
+            cos = jnp.where(left, turns[2 * d][0], turns[2 * d + 1][0])
+            sin = jnp.where(left, turns[2 * d][1], turns[2 * d + 1][1])
+            n = 2 * i + d
+            lines[pl.ds(n, MINOR, stride=both), :] = b_re * cos - b_im * sin
+            lines[pl.ds(n + slots, MINOR, stride=both), :] = b_im * cos + b_re * sin
+        return 0
+
+    lax.fori_loop(0, twist_ref.shape[0] // 4, several, 0)
+
+    def last(i, _):
+        cols = []
+        for d in range(2):
+            base = (i + d * (MINOR // 2)) * both
+            cols.append(
+                jnp.concatenate(
+                    [
+                        lines[pl.ds(pl.multiple_of(base, 8), kept), :],
+                        lines[pl.ds(pl.multiple_of(base + slots, 8), kept), :],
+                    ],
+                    axis=0,
+                )
             )
-        backs = [dot3(inv_ref, jnp.concatenate(prods[d : d + 2], axis=1)) for d in (0, 2)]
-        for d, (at_re, at_im, cos, sin, _, _) in enumerate(loaded):
-            back = backs[d // 2][:, (d % 2) * chans : (d % 2 + 1) * chans]
-            b_re, b_im = back[:MINOR], back[MINOR:]
-            sig_lines[at_re, :] = b_re * cos - b_im * sin
-            sig_lines[at_im, :] = b_im * cos + b_re * sin
-        return 0
-
-    lax.fori_loop(0, twist_ref.shape[0] // 4, several, 0)
-
-    def last(i, _):
-        cols = [
-            sig_lines[pl.ds(pl.multiple_of((2 * i + d) * both, 8), both), :] for d in range(2)
-        ]
         high, low = hi_lo(jnp.concatenate(cols, axis=1))
         got = jnp.dot(
             w2_ref[...],
             jnp.concatenate([high, low, high], axis=0),
             preferred_element_type=jnp.float32,
         )
-        for d in range(2):
-            wide_ref[pl.ds(2 * i + d, half, stride=MINOR), :] = got[:, d * chans : (d + 1) * chans]
+        early = got[:half, :chans] + swap(got[half:, :chans])
+        late = swap(got[:half, chans:]) + got[half:, chans:]
+        wide_ref[pl.ds(i, half, stride=MINOR // 2), :] = jnp.where(left, early, late)
         return 0
 
     lax.fori_loop(0, MINOR // 2, last, 0, unroll=4)
 
     def narrow(i, _):
-        at = pl.ds(pl.multiple_of(i * rows, rows), rows)
+        at = pl.ds(pl.multiple_of(i * (rows // 2), rows // 2), rows // 2)
         out_ref[i] = wide_ref[at, :].astype(jnp.bfloat16)
         return 0
 
@@ -265,12 +276,11 @@
 
 def whole_conv(both):
     devices, rows, chans = both.shape
-    rows = rows // 2
     length = devices * rows
     half = length // MINOR
     lines, span = 2 * half, 2 * length
     classes = half + 1
-    slots = -(-classes // 8) * 8
+    slots = -(-classes // 16) * 16
     cos, sin = line_tables(lines)
     w1 = np.zeros((2, slots, half))
     w1[0, :classes], w1[1, :classes] = cos, -sin
@@ -280,7 +290,10 @@
     weight /= span
     w2 = np.zeros((2, slots, half))
     w2[0, :classes], w2[1, :classes] = weight * cos, -weight * sin
-    w2 = split_table(w2.reshape(2 * slots, half).T)
+    kept = -(-slots // 16) * 8
+    paired = np.zeros((2, 2, kept, half))
+    paired[:, :, : slots // 2] = w2.reshape(2, slots // 2, 2, half).transpose(2, 0, 1, 3)
+    w2 = split_table(paired.transpose(0, 3, 1, 2).reshape(2 * half, 2 * kept))
     w1 = jnp.concatenate([w1[0], w1[1]], axis=1)
     w2 = jnp.concatenate([w2[0], w2[0], w2[1]], axis=1)
     index = np.arange(MINOR)
@@ -295,10 +308,9 @@
         conv_kernel,
         in_specs=[vmem] * 6,
         out_specs=vmem,
-        out_shape=jax.ShapeDtypeStruct((devices, rows, chans), jnp.bfloat16),
+        out_shape=jax.ShapeDtypeStruct((devices, rows // 2, chans), jnp.bfloat16),
         scratch_shapes=[
             pltpu.VMEM((length, chans), jnp.float32),
-            pltpu.VMEM((MINOR * 2 * slots, chans), jnp.float32),
             pltpu.VMEM((MINOR * 2 * slots, chans), jnp.float32),
         ],
         compiler_params=pltpu.CompilerParams(vmem_limit_bytes=48 * 1024 * 1024),
@@ -311,23 +323,29 @@
     )(w1, w2, fwd, inv, twist, both)
 
 
-def prepare_kernel(key_ref, value_ref, filter_ref, both_ref):
-    rows, each = key_ref.shape[0], both_ref.shape[2]
-    for n in range(both_ref.shape[0]):
+def prepare_kernel(key_ref, value_ref, filter_ref, *both_refs):
+    each = both_refs[0].shape[2]
+    for n in range(both_refs[0].shape[0]):
+        for h, both_ref in enumerate(both_refs):
+            at = slice(n * each + h * each // 2, n * each + (h + 1) * each // 2)
+            signal = key_ref[:, at].astype(jnp.float32) * value_ref[:, at].astype(jnp.float32)
+            both_ref[n] = jnp.concatenate(
+                [signal, filter_ref[:, at].astype(jnp.float32)], axis=1
+            ).astype(jnp.bfloat16)
+
+
+def finish_kernel(gate_ref, key_ref, value_ref, skip_ref, one_ref, two_ref, out_ref):
+    _, packed, each = one_ref.shape
+    left = lax.broadcasted_iota(jnp.int32, (1, each), 1) < each // 2
+    swap = lambda x: pltpu.roll(x, each // 2, 1)
+    for n in range(one_ref.shape[0]):
         at = slice(n * each, (n + 1) * each)
+        one, two = one_ref[n].astype(jnp.float32), two_ref[n].astype(jnp.float32)
+        lows = jnp.where(left, one, swap(two)).reshape(-1, MINOR // 2, each)
+        highs = jnp.where(left, swap(one), two).reshape(-1, MINOR // 2, each)
+        conv = jnp.concatenate([lows, highs], axis=1).reshape(2 * packed, each)
         signal = key_ref[:, at].astype(jnp.float32) * value_ref[:, at].astype(jnp.float32)
-        both_ref[n, :rows] = signal.astype(jnp.bfloat16)
-        both_ref[n, rows:] = filter_ref[:, at]
-
-
-def finish_kernel(gate_ref, key_ref, value_ref, skip_ref, conv_ref, out_ref):
-    each = conv_ref.shape[2]
-    for n in range(conv_ref.shape[0]):
-        at = slice(n * each, (n + 1) * each)
-        signal = key_ref[:, at].astype(jnp.float32) * value_ref[:, at].astype(jnp.float32)
-        out = gate_ref[:, at].astype(jnp.float32) * (
-            conv_ref[n].astype(jnp.float32) + skip_ref[:, at] * signal
-        )
+        out = gate_ref[:, at].astype(jnp.float32) * (conv + skip_ref[:, at] * signal)
         out_ref[:, at] = out.astype(jnp.bfloat16)
 
 
@@ -337,14 +355,14 @@
     step = 4 if devices % 4 == 0 else 1
     whole = pl.BlockSpec((rows, step * each), lambda i: (0, i))
     thin = pl.BlockSpec((1, step * each), lambda i: (0, i))
-    split = pl.BlockSpec((step, rows, each), lambda i: (i, 0, 0))
-    widened = pl.BlockSpec((step, 2 * rows, each), lambda i: (i, 0, 0))
+    split = lambda n: pl.BlockSpec((step, n, each), lambda i: (i, 0, 0))
+    out = jax.ShapeDtypeStruct(shape, jnp.bfloat16)
     return pl.pallas_call(
         kernel,
         grid=(devices // step,),
-        in_specs=[whole] * len(flat) + [thin] * len(rowed) + [split] * len(pieces),
-        out_specs=whole if len(shape) == 2 else widened,
-        out_shape=jax.ShapeDtypeStruct(shape, jnp.bfloat16),
+        in_specs=[whole] * len(flat) + [thin] * len(rowed) + [split(rows // 2)] * len(pieces),
+        out_specs=whole if len(shape) == 2 else [split(rows)] * 2,
+        out_shape=out if len(shape) == 2 else [out] * 2,
         compiler_params=pltpu.CompilerParams(vmem_limit_bytes=40 * 1024 * 1024),
         cost_estimate=pl.CostEstimate(
             flops=rows * chans * 4, bytes_accessed=rows * chans * 10, transcendentals=0
@@ -374,28 +392,29 @@
             (hyena_key, hyena_value, long_filter),
             (),
             (),
-            (devices, 2 * rows, each),
+            (devices, rows, each),
             devices,
             "prepare",
         )
     else:
         signal = hyena_key.astype(jnp.float32) * hyena_value.astype(jnp.float32)
         both = jnp.concatenate([signal.astype(jnp.bfloat16), long_filter], axis=0)
-        both = both.reshape(2 * rows, devices, each).transpose(1, 0, 2)
+        both = [both.reshape(2 * rows, devices, each).transpose(1, 0, 2)]
     behind, both = lax.optimization_barrier((behind, both))
-    both = exchange(both)
+    both = [exchange(x) for x in both]
     behind = lax.all_gather(behind, "chan", axis=2, tiled=True)
     tokens, groups, features = attn_query.shape
     queries = attn_query.reshape(tokens * groups, features)
+    queries, both[0] = lax.optimization_barrier((queries, both[0]))
     out, lse = attend(queries, groups, behind, own, my_index)
-    out, lse, both = lax.optimization_barrier((out, lse, both))
+    out, lse, both[0] = lax.optimization_barrier((out, lse, both[0]))
     if aligned:
-        conv = whole_conv(both)
+        conv = [whole_conv(x) for x in both]
         hyena_out = by_groups(
             finish_kernel,
             (hyena_gate, hyena_key, hyena_value),
             (skip_weight[None, :],),
-            (exchange(conv),),
+            [exchange(x) for x in conv],
             (rows, chans),
             devices,
             "finish",
@@ -403,7 +422,7 @@
     else:
         cube = (devices * rows // MINOR, MINOR, each)
         lines = 2 * cube[0]
-        sig, ker = both[:, :rows].reshape(cube), both[:, rows:].reshape(cube)
+        sig, ker = (x.reshape(cube) for x in (both[0][:, :rows], both[0][:, rows:]))
         back = spectra_product(spread(sig), spread(ker), lines * MINOR)
         conv = gather_lines(*back, lines).astype(jnp.bfloat16)
         conv = exchange(conv.reshape(devices, rows, each)).transpose(1, 0, 2).reshape(rows, chans)

time: 249 us -> 286 us (1.15)
  Pallas kernels: 86.4 us -> 118 us
  starting transfers between devices: 15.4 us -> 28.3 us
  waiting for transfers between devices: 97.9 us -> 85.4 us
  local copies, waits for them, and re-layouts: 32.6 us -> 37.6 us
    pallas_call x1 -> x2, Pallas kernels: 43.9 us -> 74.3 us  [whole_conv(): pl.pallas_call(conv_kernel, in_specs=[vmem] * 6, out_specs=vmem, out_shap...]
    all_to_all x2 -> x4, starting transfers between devices: 11.9 us -> 24.9 us  [exchange(): return lax.all_to_all(x, 'seq', split_axis=0, concat_axis=0, tiled=True)]
    all_gather x1, waiting for transfers between devices: 13.3 us -> 6.49 us  [local(): behind = lax.all_gather(behind, 'chan', axis=2, tiled=True)]
    all_gather x1, waiting for transfers between devices: 6.23 us -> 0.01 us  [local(): own = lax.all_gather(kv_pair, 'chan', axis=2, tiled=True)]
    unnamed x35 -> x43, local copies, waits for them, and re-layouts: 18.1 us -> 22.2 us
    all_to_all x2 -> x4, waiting for transfers between devices: 59.2 us -> 61.6 us  [exchange(): return lax.all_to_all(x, 'seq', split_axis=0, concat_axis=0, tiled=True)]
  transfers between devices with their start and end apart: 5 -> 7, of which waited for: 5 -> 4; matrix products, arithmetic and copies ran while one was open for 6% -> 6% of each run, Pallas kernels for 15% -> 40%
where the time goes in v4:
time: 286 us; the launch traced here: 285 us
  Pallas kernels  118 us (41%)
  waiting for transfers between devices  85.4 us (30%)
  local copies, waits for them, and re-layouts  37.6 us (13%)
  starting transfers between devices  28.3 us (10%)
  between operations  14.2 us (5%)
    pallas_call x2, Pallas kernels, whole_conv(): pl.pallas_call(conv_kernel, in_specs=[vmem] * 6, out_specs=vmem, out_shap...  74.3 us
    all_to_all x4, waiting for transfers between devices, exchange(): return lax.all_to_all(x, 'seq', split_axis=0, concat_axis=0, tiled=True)  61.6 us
    pallas_call x1, Pallas kernels, attend(): pl.pallas_call(functools.partial(attend_kernel, groups), grid=(heads,), i...  36.5 us
    all_to_all x4, starting transfers between devices, exchange(): return lax.all_to_all(x, 'seq', split_axis=0, concat_axis=0, tiled=True)  24.9 us
    unnamed x43, local copies, waits for them, and re-layouts  22.2 us
    ppermute x1, waiting for transfers between devices, local(): lax.ppermute(kv_pair, 'seq', [(i, i + 1) for i in range(devices - 1)])  16 us
    reshape x1, local copies, waits for them, and re-layouts, local(): return (hyena_out, out.reshape(attn_query.shape), attn_lse)  7.17 us
    pallas_call x2, Pallas kernels, by_groups(): pl.pallas_call(kernel, grid=(devices // step,), in_specs=[whole] * len(fl...  7.08 us
  transfers between devices with their start and end apart: 7, of which 4 were waited for; matrix products, arithmetic and copies ran while one was open for 6% of the time, Pallas kernels for 40%

profile of v4, /device:TPU:12, one launch (start us, length us, event | category | flops | bytes accessed | tf_op | source)
XLA Modules:
  0.0 284.9 jit_solution(7564117102944608520)
XLA Ops:
  7.2 1.4 pad_maximum_fusion
  8.6 3.4 %collective-permute-start = (bf16[2,512,512]{2,1,0:T(8,128)(2,1)S(1)}, bf16[2,512,512]{2,1,0:T(8,128)(2,1)}, u32[]{:S(2)}, u32[]{:S(2)}) collective-permute-start(bf16[2,512,512]{2,1,0:T(8,128)(2,1)S(1)} %pad_maximum_fusion), channel_id=1, source_target_pairs={{0,2},{2,4},{4,6},{6,8},{8,10},{10,12},{12,14},{14,16},{16,18},{18... | collective-permute-start | bytes 3145736 | tf_op jit(solution)/shard_map/ppermute | solution.py:387
  12.1 1.6 copy-done.1
  13.6 1.6 copy-done.5
  15.2 2.5 prepare.1
  17.7 1.4 copy-done.6
  19.1 1.3 copy-done.7
  20.4 16.0 %collective-permute-done = bf16[2,512,512]{2,1,0:T(8,128)(2,1)} collective-permute-done((bf16[2,512,512]{2,1,0:T(8,128)(2,1)S(1)}, bf16[2,512,512]{2,1,0:T(8,128)(2,1)}, u32[]{:S(2)}, u32[]{:S(2)}) %collective-permute-start) | collective-permute-done | bytes 1048608 | tf_op jit(solution)/shard_map/ppermute | solution.py:387
  36.4 6.3 %all-to-all-start = ((bf16[16,512,128]{2,1,0:T(8,128)(2,1)}), bf16[16,512,128]{2,1,0:T(8,128)(2,1)}, u32[]{:S(2)}, u32[]{:S(2)}) async-start(bf16[16,512,128]{2,1,0:T(8,128)(2,1)} %copy-done.7), calls=%async_computation | async-start | bytes 4194304 | tf_op jit(solution)/shard_map/all_to_all | solution.py:375
  43.4 46.9 %all-to-all-done.both_ref = bf16[16,512,128]{2,1,0:T(8,128)(2,1)} async-done(((bf16[16,512,128]{2,1,0:T(8,128)(2,1)}), bf16[16,512,128]{2,1,0:T(8,128)(2,1)}, u32[]{:S(2)}, u32[]{:S(2)}) %all-to-all-start) | async-done | bytes 2097184 | tf_op jit(solution)/shard_map/all_to_all | solution.py:375
  90.3 4.7 %all-to-all-start.2 = ((bf16[16,512,128]{2,1,0:T(8,128)(2,1)}), bf16[16,512,128]{2,1,0:T(8,128)(2,1)}, u32[]{:S(2)}, u32[]{:S(2)}) async-start(bf16[16,512,128]{2,1,0:T(8,128)(2,1)} %copy-done.6), calls=%async_computation.2 | async-start | bytes 4194304 | tf_op jit(solution)/shard_map/all_to_all | solution.py:375
  95.8 6.9 %reshape.19.q_ref = bf16[2048,1024]{1,0:T(8,128)(2,1)} reshape(bf16[512,4,1024]{2,1,0:T(4,128)(2,1)} %param.23) | data formatting | bytes 8388608 | tf_op jit(solution)/shard_map/reshape | solution.py:407
  102.7 6.5 %all-gather.3.cloned.1.call-done.kp_ref.vp_ref = bf16[2,512,1024]{2,1,0:T(8,128)(2,1)} async-done(((bf16[2,512,512]{2,1,0:T(8,128)(2,1)}), bf16[2,512,1024]{2,1,0:T(8,128)(2,1)}) %all-gather.3.cloned.1.call-update) | async-done | bytes 2097168 | tf_op jit(solution)/shard_map/all_gather | solution.py:405
  109.2 2.2 copy-done.4
  111.4 1.6 copy-done.12
  112.9 1.6 copy-done.13
  114.5 36.5 %attend.1 = (bf16[2048,1024]{1,0:T(8,128)(2,1)S(1)}, f32[8,1,2048]{2,1,0:T(1,128)S(1)}) custom-call(f32[1,1]{1,0:T(1,128)} %bitcast.1.bias_ref, bf16[2048,1024]{1,0:T(8,128)(2,1)S(1)} %copy-done.4, bf16[2,512,1024]{2,1,0:T(8,128)(2,1)S(1)} %copy-done.13, bf16[2,512,1024]{2,1,0:T(8,128)(2,1)S(1)} %copy-done.13, bf16[2,512,1024]{2,1,0:T(8,128)(2,1)S(1)} %copy-done.12, ...), custom_call_target="tpu_custom_call" | custom-call | flops 8589934592 | bytes 12582912 | tf_op jit(solution)/shard_map/attend/pallas_call | solution.py:155
  151.1 2.0 copy-done.3
  153.1 37.2 %whole_conv.2 = bf16[16,256,128]{2,1,0:T(8,128)(2,1)S(1)} custom-call(bf16[160,128]{1,0:T(8,128)(2,1)S(1)} %copy-done.18, bf16[128,240]{1,0:T(8,128)(2,1)S(1)} %copy-done.17, bf16[2,256,256]{2,1,0:T(8,128)(2,1)S(1)} %copy-done.15, bf16[2,256,256]{2,1,0:T(8,128)(2,1)S(1)} %copy-done.14, f32[68,128,2]{2,1,0:T(8,128)} %constant.26.clone.twist_ref, ...), custom_call_target="tpu_custom_call" | custom-call | flops 9814671360 | bytes 6291456 | tf_op jit(solution)/shard_map/whole_conv/pallas_call | solution.py:307
  190.3 1.0 copy-done.10
  191.2 7.0 %all-to-all-start.1 = ((bf16[16,256,128]{2,1,0:T(8,128)(2,1)}), bf16[16,256,128]{2,1,0:T(8,128)(2,1)S(1)}, u32[]{:S(2)}, u32[]{:S(2)}) async-start(bf16[16,256,128]{2,1,0:T(8,128)(2,1)} %copy-done.10), calls=%async_computation.1 | async-start | bytes 2097152 | tf_op jit(solution)/shard_map/all_to_all | solution.py:375
  198.2 0.9 copy-done.16
  199.9 37.1 %whole_conv.3 = bf16[16,256,128]{2,1,0:T(8,128)(2,1)S(1)} custom-call(bf16[160,128]{1,0:T(8,128)(2,1)S(1)} %copy-done.19, bf16[128,240]{1,0:T(8,128)(2,1)S(1)} %copy-done.17, bf16[2,256,256]{2,1,0:T(8,128)(2,1)S(1)} %copy-done.16, bf16[2,256,256]{2,1,0:T(8,128)(2,1)S(1)} %copy-done.14, f32[68,128,2]{2,1,0:T(8,128)} %constant.26.clone.twist_ref, ...), custom_call_target="tpu_custom_call" | custom-call | flops 9814671360 | bytes 6291456 | tf_op jit(solution)/shard_map/whole_conv/pallas_call | solution.py:307
  237.0 1.0 copy-done.9
  238.0 6.9 %all-to-all-start.3 = ((bf16[16,256,128]{2,1,0:T(8,128)(2,1)}), bf16[16,256,128]{2,1,0:T(8,128)(2,1)}, u32[]{:S(2)}, u32[]{:S(2)}) async-start(bf16[16,256,128]{2,1,0:T(8,128)(2,1)} %copy-done.9), calls=%async_computation.3 | async-start | bytes 2097152 | tf_op jit(solution)/shard_map/all_to_all | solution.py:375
  244.9 1.3 copy.22
  246.3 2.2 copy.23
  248.4 7.2 %reshape.20 = bf16[512,4,1024]{2,1,0:T(4,128)(2,1)} reshape(bf16[2048,1024]{1,0:T(8,128)(2,1)} %copy-done.3) | data formatting | bytes 8388608 | tf_op jit(solution)/shard_map/reshape | solution.py:435
  255.6 14.7 %all-to-all-done.3.two_ref = bf16[16,256,128]{2,1,0:T(8,128)(2,1)} async-done(((bf16[16,256,128]{2,1,0:T(8,128)(2,1)}), bf16[16,256,128]{2,1,0:T(8,128)(2,1)}, u32[]{:S(2)}, u32[]{:S(2)}) %all-to-all-start.3) | async-done | bytes 1048608 | tf_op jit(solution)/shard_map/all_to_all | solution.py:375
  270.3 1.6 copy-done.2
  271.9 1.6 copy-done.8
  273.5 4.6 %finish.1 = bf16[512,2048]{1,0:T(8,128)(2,1)} custom-call(bf16[512,2048]{1,0:T(8,128)(2,1)S(1)} %copy-done.8, bf16[512,2048]{1,0:T(8,128)(2,1)S(1)} %copy-done, bf16[512,2048]{1,0:T(8,128)(2,1)S(1)} %copy-done.2, f32[1,2048]{1,0:T(1,128)S(1)} %bitcast.7, bf16[16,256,128]{2,1,0:T(8,128)(2,1)S(1)} %all-to-all-done.1.one_ref, ...), custom_call_target="tpu_custom_call" | custom-call | flops 4194304 | bytes 10485760 | tf_op jit(solution)/shard_map/finish/pallas_call | solution.py:360
  (36 shorter events, 2.3 us)
Async XLA Ops:
  7.2 4.9 %copy-start = (bf16[512,2048]{1,0:T(8,128)(2,1)S(1)}, bf16[512,2048]{1,0:T(8,128)(2,1)}, u32[]{:S(2)}) copy-start(bf16[512,2048]{1,0:T(8,128)(2,1)} %key_ref.3) | copy-start | bytes 6291460
  8.6 9.1 %copy-start.20 = (bf16[2,512,512]{2,1,0:T(8,128)(2,1)}, bf16[2,512,512]{2,1,0:T(8,128)(2,1)S(1)}, u32[]{:S(2)}) copy-start(bf16[2,512,512]{2,1,0:T(8,128)(2,1)S(1)} %pad_maximum_fusion) | copy-start | bytes 3145732
  8.6 27.8 %collective-permute-start = (bf16[2,512,512]{2,1,0:T(8,128)(2,1)S(1)}, bf16[2,512,512]{2,1,0:T(8,128)(2,1)}, u32[]{:S(2)}, u32[]{:S(2)}) collective-permute-start(bf16[2,512,512]{2,1,0:T(8,128)(2,1)S(1)} %pad_maximum_fusion), channel_id=1, source_target_pairs={{0,2},{2,4},{4,6},{6,8},{8,10},{10,12},{12,14},{14,16},{16,18},{18... | collective-permute-start | bytes 3145736 | tf_op jit(solution)/shard_map/ppermute | solution.py:387
  12.1 1.6 copy-start.1
  13.6 1.6 copy-start.5
  17.7 1.4 copy-start.6
  19.1 1.3 copy-start.7
  36.4 53.9 %all-to-all-start = ((bf16[16,512,128]{2,1,0:T(8,128)(2,1)}), bf16[16,512,128]{2,1,0:T(8,128)(2,1)}, u32[]{:S(2)}, u32[]{:S(2)}) async-start(bf16[16,512,128]{2,1,0:T(8,128)(2,1)} %copy-done.7), calls=%async_computation | async-start | bytes 4194304 | tf_op jit(solution)/shard_map/all_to_all | solution.py:375
  42.7 60.0 %all-gather.5.cloned.1.call-start = ((), (), s32[]{:S(2)}) async-start(), calls=%async_computation.5 | async-start | bytes 3145728 | tf_op jit(solution)/shard_map/all_gather | solution.py:388
  90.3 100.9 %all-to-all-start.2 = ((bf16[16,512,128]{2,1,0:T(8,128)(2,1)}), bf16[16,512,128]{2,1,0:T(8,128)(2,1)}, u32[]{:S(2)}, u32[]{:S(2)}) async-start(bf16[16,512,128]{2,1,0:T(8,128)(2,1)} %copy-done.6), calls=%async_computation.2 | async-start | bytes 4194304 | tf_op jit(solution)/shard_map/all_to_all | solution.py:375
  95.0 14.1 %all-gather.3.cloned.1.call-start = ((), (), s32[]{:S(2)}) async-start(), calls=%async_computation.4 | async-start | bytes 3145728 | tf_op jit(solution)/shard_map/all_gather | solution.py:405
  109.2 2.2 copy-start.4
  111.4 1.6 copy-start.12
  112.9 1.6 copy-start.13
  114.5 38.5 %copy-start.14 = (bf16[2,256,256]{2,1,0:T(8,128)(2,1)S(1)}, bf16[2,256,256]{2,1,0:T(8,128)(2,1)}, u32[]{:S(2)}) copy-start(bf16[2,256,256]{2,1,0:T(8,128)(2,1)} %constant.25.clone.inv_ref) | copy-start | bytes 786436
  114.5 38.5 %copy-start.15 = (bf16[2,256,256]{2,1,0:T(8,128)(2,1)S(1)}, bf16[2,256,256]{2,1,0:T(8,128)(2,1)}, u32[]{:S(2)}) copy-start(bf16[2,256,256]{2,1,0:T(8,128)(2,1)} %constant.24.clone.fwd_ref) | copy-start | bytes 786436
  114.5 38.5 %copy-start.17 = (bf16[128,240]{1,0:T(8,128)(2,1)S(1)}, bf16[128,240]{1,0:T(8,128)(2,1)}, u32[]{:S(2)}) copy-start(bf16[128,240]{1,0:T(8,128)(2,1)} %constant.36.w2_ref) | copy-start | bytes 184324
  114.5 38.5 %copy-start.18 = (bf16[160,128]{1,0:T(8,128)(2,1)S(1)}, bf16[160,128]{1,0:T(8,128)(2,1)}, u32[]{:S(2)}) copy-start(bf16[160,128]{1,0:T(8,128)(2,1)} %constant.31.w1_ref) | copy-start | bytes 122884
  151.1 2.0 copy-start.3
  190.3 1.0 copy-start.10
  191.2 46.8 %all-to-all-start.1 = ((bf16[16,256,128]{2,1,0:T(8,128)(2,1)}), bf16[16,256,128]{2,1,0:T(8,128)(2,1)S(1)}, u32[]{:S(2)}, u32[]{:S(2)}) async-start(bf16[16,256,128]{2,1,0:T(8,128)(2,1)} %copy-done.10), calls=%async_computation.1 | async-start | bytes 2097152 | tf_op jit(solution)/shard_map/all_to_all | solution.py:375
  198.2 0.9 copy-start.16
  199.2 0.8 copy-start.19
  237.0 1.0 copy-start.9
  238.0 32.3 %all-to-all-start.3 = ((bf16[16,256,128]{2,1,0:T(8,128)(2,1)}), bf16[16,256,128]{2,1,0:T(8,128)(2,1)}, u32[]{:S(2)}, u32[]{:S(2)}) async-start(bf16[16,256,128]{2,1,0:T(8,128)(2,1)} %copy-done.9), calls=%async_computation.3 | async-start | bytes 2097152 | tf_op jit(solution)/shard_map/all_to_all | solution.py:375
  248.4 21.9 %copy-start.11 = (f32[2048]{0:T(1024)S(1)}, f32[2048]{0:T(1024)}, u32[]{:S(2)}) copy-start(f32[2048]{0:T(1024)} %param.22) | copy-start | bytes 24580
  270.3 1.6 copy-start.2
  271.9 1.6 copy-start.8
Sparse Core Ops, SparseCore 0:
  45.1 11.6 all-gather.4
  97.4 11.6 all-gather.2
